TPU v7x, 256 devices: a whole 4x4x8 slice. The times are simulated.
256 devices in a mesh: stn: 128 (over z, x_lo, y, core), tm: 2 (over x_hi).
Axes of the slice: x: 4 (x_hi: 2, x_lo: 2; x = x_hi * 2 + x_lo), y: 4, z: 8, core: 2. Of those that a mesh axis runs over, the one named last changes fastest.
Arguments:
- samples: bfloat16 [512, 2, 2, 131072], P('stn', None, None, 'tm'), may hold values from -6 to 6
- taps: float32 [12, 4096], replicated, may hold values from -1.8 to 1.8
- codes: int32 [64, 512], replicated, may hold values from 0 to 4095
- flags: int32 [512], replicated, may hold values 0 or 1
Outputs:
- beams: bfloat16 [4096, 2, 32, 128], P('stn', None, 'tm')
All inputs are finite; a program needn't handle non-finite values.
Results may differ from a plain program's by a relative error of at most 0.0077.
Values may be sent and summed in bfloat16 or wider, within the bound.
No kernel may reach another device: no remote copies, remote signals or barrier semaphores. Data moves between devices by JAX's collectives and lax.ppermute only.
A program may use at most 64 MiB of HBM per device.

v0:
```python
import jax
import jax.numpy as jnp
from jax import lax
from jax.sharding import PartitionSpec as P

RADIX_A = 32
RADIX_B = 128


def from_behind(shard, axis, by):
    size = lax.axis_size(axis)
    pairs = [(i, i + by) for i in range(size) if 0 <= i + by < size]
    return lax.ppermute(shard, axis, pairs)


def dft_table(radix):
    indices = jnp.arange(radix, dtype=jnp.int32)
    angles = (indices[:, None] * indices[None, :] % radix).astype(jnp.float32) * (
        2.0 * jnp.pi / radix
    )
    cosine = jnp.cos(angles).astype(jnp.bfloat16)
    sine = jnp.sin(angles).astype(jnp.bfloat16)
    return jnp.stack(
        [jnp.stack([cosine, -sine], axis=1), jnp.stack([sine, cosine], axis=1)], axis=0
    )


def twiddle_table(outer, inner):
    length = outer * inner
    rows = jnp.arange(outer, dtype=jnp.int32)
    cols = jnp.arange(inner, dtype=jnp.int32)
    angles = (rows[:, None] * cols[None, :] % length).astype(jnp.float32) * (2.0 * jnp.pi / length)
    return (jnp.cos(angles), jnp.sin(angles))


def beam_weights(codes, flags, channels, length, stations_all):
    phase = channels[:, :, None, None] * jnp.transpose(codes)[None, None, :, :] % length
    angles = phase.astype(jnp.float32) * (2.0 * jnp.pi / length)
    scale = flags.astype(jnp.float32) / jnp.sqrt(jnp.float32(stations_all))
    real_part = (jnp.cos(angles) * scale[None, None, :, None]).astype(jnp.bfloat16)
    imag_part = (-jnp.sin(angles) * scale[None, None, :, None]).astype(jnp.bfloat16)
    first_row = jnp.stack([real_part, imag_part], axis=3)
    second_row = jnp.stack([-imag_part, real_part], axis=3)
    return jnp.stack([first_row, second_row], axis=2)


def shards(samples, taps, codes, flags):
    stn_local = samples.shape[0]
    tap_count = taps.shape[0]
    length = taps.shape[1]
    outer = RADIX_A
    inner = RADIX_B
    frame_count = samples.shape[3] // length
    frames = samples.reshape(stn_local, 2, 2, frame_count, outer, inner)
    history = from_behind(frames[:, :, :, frame_count - (tap_count - 1) :], "tm", 1)
    padded = jnp.concatenate([history, frames], axis=3)
    taps_grid = taps.reshape(tap_count, outer, inner)
    filtered = jnp.zeros((stn_local, 2, 2, frame_count, outer, inner), jnp.float32)
    for tap in range(tap_count):
        filtered = filtered + taps_grid[tap][None, None, None, None] * padded[
            :, :, :, tap : tap + frame_count
        ].astype(jnp.float32)
    filtered = filtered.astype(jnp.bfloat16)
    table_outer = dft_table(outer)
    table_inner = dft_table(inner).reshape(2 * inner, 2 * inner)
    tw_cos, tw_sin = twiddle_table(outer, inner)
    tw_cos = tw_cos[:, None, None, None, :]
    tw_sin = tw_sin[:, None, None, None, :]
    norm = jnp.sqrt(jnp.float32(length))
    first = jnp.einsum(
        "iaoc,spifab->ocspfb", table_outer, filtered, preferred_element_type=jnp.float32
    )
    real_in = first[0]
    imag_in = first[1]
    real_out = (real_in * tw_cos + imag_in * tw_sin) / norm
    imag_out = (imag_in * tw_cos - real_in * tw_sin) / norm
    middle = jnp.concatenate([real_out, imag_out], axis=-1).astype(jnp.bfloat16)
    second = jnp.einsum("cspfk,kn->cspfn", middle, table_inner, preferred_element_type=jnp.float32)
    spectra = second.astype(jnp.bfloat16).reshape(outer, stn_local, 2, frame_count, 2, inner)
    digits = inner // lax.axis_size("stn")
    upper = lax.axis_index("stn") * digits + jnp.arange(digits, dtype=jnp.int32)
    channels = jnp.arange(outer, dtype=jnp.int32)[None, :] + outer * upper[:, None]
    stations_all = codes.shape[1]
    beam_count = codes.shape[0]
    weights = beam_weights(codes, flags, channels, length, stations_all)
    turned = lax.all_to_all(spectra, "stn", split_axis=5, concat_axis=1, tiled=True)
    result = jnp.einsum(
        "cspfoe,ecosrb->ecpfrb", turned, weights, preferred_element_type=jnp.float32
    )
    return result.reshape(digits * outer, 2, turned.shape[3], 2 * beam_count).astype(jnp.bfloat16)


def solution(mesh):
    in_specs = (P("stn", None, None, "tm"), P(), P(), P())
    out_specs = P("stn", None, "tm", None)
    return jax.shard_map(shards, mesh=mesh, in_specs=in_specs, out_specs=out_specs, check_vma=False)
```

profile of v0, /device:TPU:7, one launch (start us, length us, event | category | flops | bytes accessed | tf_op | source)
XLA Modules:
  0.0 171.2 jit_solution(11299359552949289476)
XLA Ops:
  0.0 4.9 %reshape.358 = bf16[4,2,2,16,32,128]{5,4,3,2,1,0:T(8,128)(2,1)S(1)} reshape(bf16[4,2,2,65536]{3,2,1,0:T(2,128)(2,1)} %param.4) | data formatting | bytes 4194304 | tf_op jit(solution)/shard_map/reshape | solution.py:54
  4.9 0.3 slice.116
  5.2 0.4 copy.57
  5.6 1.3 collective-permute-start
  6.9 0.3 sine_convert_fusion
  7.2 0.3 fusion.35
  7.5 0.8 copy.34
  8.3 1.6 reshape.366
  10.0 0.1 fusion.38
  10.0 0.1 sine_convert_fusion.1
  10.1 0.1 fusion.36
  10.2 2.0 %fusion.43 = (f32[1,4096]{1,0:T(1,128)S(1)}, f32[1,4096]{1,0:T(1,128)S(1)}, f32[1,4096]{1,0:T(1,128)S(1)}, f32[1,4096]{1,0:T(1,128)S(1)}, f32[1,4096]{1,0:T(1,12...) fusion(f32[12,4096]{1,0:T(8,128)} %param.5), kind=kLoop, calls=%fused_computation.81 | loop fusion | bytes 393216 | tf_op jit(solution)/shard_map/slice | solution.py:60
  12.2 29.3 %collective-permute-done = bf16[4,2,2,11,32,128]{5,4,2,3,1,0:T(8,128)(2,1)} collective-permute-done((bf16[4,2,2,11,32,128]{5,4,2,3,1,0:T(8,128)(2,1)S(1)}, bf16[4,2,2,11,32,128]{5,4,2,3,1,0:T(8,128)(2,1)}, u32[]{:S(2)}, u32[]{:S(2)}) %collective-permute-start) | collective-permute-done | bytes 1441824 | tf_op jit(solution)/shard_map/ppermute | solution.py:13
  41.6 1.8 %constant_dynamic-update-slice_fusion.1 = bf16[4,2,2,27,32,128]{5,4,2,3,1,0:T(8,128)(2,1)S(1)} fusion(bf16[4,2,2,11,32,128]{5,4,2,3,1,0:T(8,128)(2,1)} %collective-permute-done), kind=kLoop, calls=%fused_computation.73 | loop fusion | bytes 2883584
  43.4 0.8 constant_dynamic-update-slice_fusion
  44.2 4.6 %convolution_bitcast_fusion = f32[2,32,4,2,16,128]{5,1,4,3,2,0:T(8,128)S(1)} fusion(bf16[4,2,2,27,32,128]{5,4,2,3,1,0:T(8,128)(2,1)S(1)} %constant_dynamic-update-slice_fusion, f32[32,128]{1,0:T(8,128)S(1)} %bitcast.96, f32[32,128]{1,0:T(8,128)S(1)} %bitcast.97, f32[32,128]{1,0:T(8,128)S(1)} %bitcast.87, f32[32,128]{1,0:T(8,128)S(1)} %bitcast.88, ...), kind=kOutput, calls=%fused_computation.17 | convolution fusion | flops 171982848 | bytes 29589504 | tf_op jit(solution)/shard_map/iaoc,spifab->ocspfb/dot_general | solution.py:70
  48.8 0.7 multiply_convert_fusion.3
  49.5 0.3 pad_maximum_fusion
  49.8 3.8 %fusion.9 = bf16[32,4,2,16,256]{4,3,2,1,0:T(8,128)(2,1)} fusion(bf16[32,4,2,16,256]{4,0,3,2,1:T(8,128)(2,1)S(1)} %pad_maximum_fusion, bf16[256,256,1,1,1]{1,0,2,3,4:T(8,128)(2,1)S(1)} %copy-done.1), kind=kOutput, calls=%fused_computation.26 | convolution fusion | flops 537919488 | bytes 4325376 | tf_op jit(solution)/shard_map/cspfk,kn->cspfn/dot_general | solution.py:78
  53.6 2.5 %reshape.360 = bf16[32,4,2,16,2,128]{5,4,3,2,1,0:T(2,128)(2,1)S(1)} reshape(bf16[32,4,2,16,256]{4,3,2,1,0:T(8,128)(2,1)} %fusion.9) | data formatting | bytes 4194304 | tf_op jit(solution)/shard_map/reshape | solution.py:79
  56.2 11.0 %copy.36 = bf16[32,4,2,16,2,128]{0,3,4,2,1,5:T(8,128)(2,1)} copy(bf16[32,4,2,16,2,128]{5,4,3,2,1,0:T(2,128)(2,1)S(1)} %reshape.360) | data formatting | bytes 4194304 | tf_op jit(solution)/shard_map/reshape | solution.py:79
  67.2 12.8 %reshape.371 = bf16[128,2,4096]{2,1,0:T(2,128)(2,1)} reshape(bf16[128,4,2,2,16,32]{5,4,3,2,1,0:T(8,128)(2,1)} %bitcast.82) | data formatting | bytes 4194304
  80.0 15.2 %all-to-all-start = ((bf16[128,2,4096]{2,1,0:T(2,128)(2,1)}), bf16[128,2,4096]{2,1,0:T(2,128)(2,1)S(1)}, u32[]{:S(2)}, u32[]{:S(2)}) async-start(bf16[128,2,4096]{2,1,0:T(2,128)(2,1)} %reshape.371), calls=%async_computation | async-start | bytes 4194304 | tf_op jit(solution)/shard_map/all_to_all | solution.py:86
  95.3 16.5 %fusion.41 = bf16[1,32,512,1,64]{2,4,3,1,0:T(8,128)(2,1)S(1)} fusion(f32[512]{0:T(512)S(1)} %convert_multiply_fusion, s32[512,64]{0,1:T(8,128)S(1)} %bitcast.84, s32[32]{0:T(128)S(1)} %iota_add_fusion), kind=kLoop, calls=%fused_computation.79 | loop fusion | flops 20971520 | bytes 2230400 | tf_op jit(solution)/shard_map/neg | solution.py:43
  111.8 17.7 %multiply_convert_fusion = (bf16[1,32,512,1,64]{2,4,3,1,0:T(8,128)(2,1)S(1)}, bf16[1,32,512,1,64]{2,4,3,1,0:T(8,128)(2,1)S(1)}) fusion(f32[512]{0:T(512)S(1)} %convert_multiply_fusion, s32[512,64]{0,1:T(8,128)S(1)} %bitcast.85, s32[32]{0:T(128)S(1)} %iota_add_fusion), kind=kLoop, calls=%fused_computation.14 | loop fusion | flops 19922944 | bytes 4327552 | tf_op jit(solution)/shard_map/convert_element_type | solution.py:41
  129.6 3.5 %maximum_bitcast_fusion.2 = (bf16[1,32,1,512,2,64]{3,5,2,4,1,0:T(8,128)(2,1)}, bf16[1,32,1,512,2,64]{3,5,2,4,1,0:T(8,128)(2,1)}) fusion(bf16[1,32,512,1,64]{2,4,3,1,0:T(8,128)(2,1)S(1)} %get-tuple-element.21, bf16[1,32,512,1,64]{2,4,3,1,0:T(8,128)(2,1)S(1)} %get-tuple-element.22, bf16[1,32,512,1,64]{2,4,3,1,0:T(8,128)(2,1)S(1)} %fusion.41), kind=kLoop, calls=%fused_computation.12 | loop fusion | flops 4194304 | bytes 14680064 | tf_op jit(solution)/shard_map/stack | solution.py:44
  133.1 14.0 %all-to-all-done = bf16[128,2,4096]{2,1,0:T(2,128)(2,1)S(1)} async-done(((bf16[128,2,4096]{2,1,0:T(2,128)(2,1)}), bf16[128,2,4096]{2,1,0:T(2,128)(2,1)S(1)}, u32[]{:S(2)}, u32[]{:S(2)}) %all-to-all-start) | async-done | bytes 2097184 | tf_op jit(solution)/shard_map/all_to_all | solution.py:86
  147.1 6.6 %reshape.372 = bf16[128,4,2,2,16,32]{5,4,3,2,1,0:T(8,128)(2,1)} reshape(bf16[128,2,4096]{2,1,0:T(2,128)(2,1)S(1)} %all-to-all-done) | data formatting | bytes 4194304
  153.7 9.6 %copy.43 = bf16[32,512,2,16,2,1]{1,3,4,5,2,0:T(8,128)(2,1)S(1)} copy(bf16[32,512,2,16,2,1]{0,3,4,2,1,5:T(8,128)(2,1)} %bitcast.83) | data formatting | bytes 4194304 | tf_op jit(solution)/shard_map/reshape.34
  163.3 6.4 %fusion.13 = bf16[32,2,16,2,64]{4,2,3,1,0:T(8,128)(2,1)S(1)} fusion(bf16[32,512,2,16,2,1]{1,3,4,5,2,0:T(8,128)(2,1)S(1)} %copy.43, bf16[1,32,1,512,2,64]{3,5,2,4,1,0:T(8,128)(2,1)} %get-tuple-element.8, bf16[1,32,1,512,2,64]{3,5,2,4,1,0:T(8,128)(2,1)} %get-tuple-element.7), kind=kOutput, calls=%fused_computation.28 | convolution fusion | flops 285343744 | bytes 10747904 | tf_op jit(solution)/shard_map/cspfoe,ecosrb->ecpfrb/dot_general | solution.py:87
  169.7 0.5 copy.39
  170.3 1.0 convert_element_type.249
  (11 shorter events, 0.1 us)
Async XLA Ops:
  5.6 36.0 %collective-permute-start = (bf16[4,2,2,11,32,128]{5,4,2,3,1,0:T(8,128)(2,1)S(1)}, bf16[4,2,2,11,32,128]{5,4,2,3,1,0:T(8,128)(2,1)}, u32[]{:S(2)}, u32[]{:S(2)}) collective-permute-start(bf16[4,2,2,11,32,128]{5,4,2,3,1,0:T(8,128)(2,1)S(1)} %copy.57), channel_id=1, source_target_pairs={{0,1},{2,3},{4,5},{6,7},{8,9},{10,11},{12,13},{14,15},{16,17},{18,... | collective-permute-start | bytes 4325384 | tf_op jit(solution)/shard_map/ppermute | solution.py:13
  48.8 1.1 copy-start.1
  80.0 15.2 %copy-start.2 = (s32[512]{0:T(512)S(1)}, s32[512]{0:T(512)}, u32[]{:S(2)}) copy-start(s32[512]{0:T(512)} %param.7) | copy-start | bytes 6148
  80.0 15.3 %copy-start = (s32[64,512]{1,0:T(8,128)S(1)}, s32[64,512]{1,0:T(8,128)}, u32[]{:S(2)}) copy-start(s32[64,512]{1,0:T(8,128)} %param.6) | copy-start | bytes 393220
  80.0 67.0 %all-to-all-start = ((bf16[128,2,4096]{2,1,0:T(2,128)(2,1)}), bf16[128,2,4096]{2,1,0:T(2,128)(2,1)S(1)}, u32[]{:S(2)}, u32[]{:S(2)}) async-start(bf16[128,2,4096]{2,1,0:T(2,128)(2,1)} %reshape.371), calls=%async_computation | async-start | bytes 4194304 | tf_op jit(solution)/shard_map/all_to_all | solution.py:86
where the time goes:
time: 172 us; the launch traced here: 171 us
  local copies, waits for them, and re-layouts  56.7 us (33%)
  waiting for transfers between devices  43.3 us (25%)
  other arithmetic  39.7 us (23%)
  starting transfers between devices  16.5 us (10%)
  matrix products  14.8 us (9%)
    ppermute x1, waiting for transfers between devices, from_behind(): return lax.ppermute(shard, axis, pairs)  29.3 us
    unnamed x10, local copies, waits for them, and re-layouts  21.6 us
    convert_element_type x1, other arithmetic, beam_weights(): (-jnp.sin(angles) * scale[None, None, :, None]).astype(jnp.bfloat16)  17.7 us
    neg x1, other arithmetic, beam_weights(): second_row = jnp.stack([-imag_part, real_part], axis=3)  16.5 us
    all_to_all x1, starting transfers between devices, shards(): lax.all_to_all(spectra, 'stn', split_axis=5, concat_axis=1, tiled=True)  15.2 us
    all_to_all x1, waiting for transfers between devices, shards(): lax.all_to_all(spectra, 'stn', split_axis=5, concat_axis=1, tiled=True)  14 us
    reshape x2, local copies, waits for them, and re-layouts, shards(): second.astype(jnp.bfloat16)  13.6 us
    another operation x1, local copies, waits for them, and re-layouts  9.62 us
  transfers between devices with their start and end apart: 2, of which 2 were waited for; matrix products, arithmetic and copies ran while one was open for 25% of the time, Pallas kernels for 0%

commit v1 on v0

v1 whole, which is shorter than its diff:
```python
import functools

import jax
import jax.numpy as jnp
import ml_dtypes
import numpy as np
from jax import lax
from jax.experimental import pallas as pl
from jax.experimental.pallas import tpu as pltpu
from jax.sharding import PartitionSpec as P

RADIX_A = 32
RADIX_B = 128
TAPS = 12
LENGTH = RADIX_A * RADIX_B
ROWS = 2 * RADIX_A
QUAD = 4
BF16 = jnp.bfloat16
F32 = jnp.float32
VMEM_LIMIT = 48 << 20


def dft_table(radix):
    indices = np.arange(radix)
    angles = (indices[:, None] * indices[None, :] % radix) * (2.0 * np.pi / radix)
    cosine = np.cos(angles).astype(ml_dtypes.bfloat16)
    sine = np.sin(angles).astype(ml_dtypes.bfloat16)
    return np.stack(
        [np.stack([cosine, -sine], axis=1), np.stack([sine, cosine], axis=1)], axis=0
    )


def outer_table():
    table = dft_table(RADIX_A)
    grid = np.zeros((2, RADIX_A, QUAD, QUAD, RADIX_A, 2), ml_dtypes.bfloat16)
    for i in range(QUAD):
        grid[:, :, i, i] = table.transpose(2, 3, 1, 0)
    return grid.reshape(2 * RADIX_A * QUAD, QUAD * ROWS)


def inner_table():
    return dft_table(RADIX_B).reshape(2 * RADIX_B, 2 * RADIX_B).T.copy()


def twiddles():
    c1 = np.repeat(np.arange(RADIX_A), QUAD)
    angles = (c1[:, None] * np.arange(RADIX_B)[None, :] % LENGTH) * (2.0 * np.pi / LENGTH)
    scale = 1.0 / np.sqrt(np.float64(LENGTH))
    return np.stack([np.cos(angles) * scale, np.sin(angles) * scale]).astype(np.float32)


def channelise_body(first, count, quads, *refs):
    if first < TAPS - 1:
        x_ref, halo_ref, taps_ref, outer_ref, tw_ref, inner_ref, out_ref, taps2, filt, mid, turn = refs
    else:
        x_ref, taps_ref, outer_ref, tw_ref, inner_ref, out_ref, taps2, filt, mid, turn = refs
        halo_ref = None
    station = pl.program_id(0)
    groups = quads
    block = 8 * groups

    @pl.when(station == 0)
    def _():
        for a in range(RADIX_A):
            for k in range(TAPS):
                row = taps_ref[k : k + 1, a * RADIX_B : (a + 1) * RADIX_B]
                taps2[k, 2 * a : 2 * a + 2, :] = jnp.broadcast_to(row, (2, RADIX_B))

    def fir(step, carry):
        pol = step // (ROWS // 16)
        row = pl.multiple_of(step % (ROWS // 16) * 16, 16)
        frames = []
        for f in range(first - TAPS + 1, first + count):
            if f < 0:
                at = pl.multiple_of((f + TAPS - 1) * ROWS + row, 16)
                piece = halo_ref[0, pol, pl.ds(at, 16), :]
            else:
                at = pl.multiple_of(f * ROWS + row, 16)
                piece = x_ref[0, pol, pl.ds(at, 16), :]
            frames.append(piece.astype(F32))
        taps = [taps2[k, pl.ds(row, 16), :] for k in range(TAPS)]
        halves = []
        for half in range(2):
            rows = slice(8 * half, 8 * half + 8)
            outs = []
            for t in range(count):
                total = taps[0][rows] * frames[t][rows]
                for k in range(1, TAPS):
                    total = total + taps[k][rows] * frames[t + k][rows]
                outs.append(total)
            halves.append(outs)
        for t in range(count):
            both = jnp.concatenate([halves[0][t], halves[1][t]], axis=0).astype(BF16)
            at = pl.multiple_of((pol * count + t) * ROWS + row, 16)
            filt[pl.ds(at, 16), :] = both
        return carry

    lax.fori_loop(0, 2 * (ROWS // 16), fir, 0)

    cosine = tw_ref[0]
    sine = tw_ref[1]
    half = RADIX_A * QUAD
    for q in range(quads):
        data = filt[q * QUAD * ROWS : (q + 1) * QUAD * ROWS, :]
        got = jnp.dot(outer_ref[...], data, preferred_element_type=F32)
        real = got[:half]
        imag = got[half:]
        real_out = (real * cosine + imag * sine).astype(BF16)
        imag_out = (imag * cosine - real * sine).astype(BF16)
        for g in range(half // 16):
            at = (g * quads + q) * 16
            mid[at : at + 16, :RADIX_B] = real_out[16 * g : 16 * g + 16]
            mid[at : at + 16, RADIX_B:] = imag_out[16 * g : 16 * g + 16]

    for pair in range(groups // 2):
        data = mid[pair * 256 : pair * 256 + 256, :]
        got = lax.dot_general(
            inner_ref[...], data, (((1,), (1,)), ((), ())), preferred_element_type=F32
        )
        for side in range(2):
            group = 2 * pair + side
            for part in range(2):
                for c in range(0, RADIX_B, 8):
                    start = c * block + group * 8 + part + 2 * station
                    turn[pl.ds(start, 8, stride=block), :] = got[
                        part * RADIX_B + c : part * RADIX_B + c + 8,
                        side * 128 : side * 128 + 128,
                    ]

    @pl.when(station == pl.num_programs(0) - 1)
    def _():
        def turn_out(step, carry):
            at = pl.multiple_of(step * 256, 256)
            out_ref[pl.ds(at, 256), :] = turn[pl.ds(at, 256), :].astype(BF16)
            return carry

        lax.fori_loop(0, RADIX_B * block // 256, turn_out, 0)


def channelise(x, halo, taps, tables, first, count):
    stations = x.shape[0]
    quads = 2 * count // QUAD
    rows = RADIX_B * 8 * quads

    def whole(array):
        return pl.BlockSpec(array.shape, lambda s: (0,) * array.ndim)

    operands = [x]
    in_specs = [pl.BlockSpec((1,) + x.shape[1:], lambda s: (s, 0, 0, 0))]
    if halo is not None:
        operands.append(halo)
        in_specs.append(pl.BlockSpec((1,) + halo.shape[1:], lambda s: (s, 0, 0, 0)))
    for array in (taps,) + tables:
        operands.append(array)
        in_specs.append(whole(array))
    return pl.pallas_call(
        functools.partial(channelise_body, first, count, quads),
        grid=(stations,),
        out_shape=jax.ShapeDtypeStruct((rows, 128), BF16),
        in_specs=in_specs,
        out_specs=pl.BlockSpec((rows, 128), lambda s: (0, 0)),
        scratch_shapes=[
            pltpu.VMEM((TAPS, ROWS, RADIX_B), F32),
            pltpu.VMEM((2 * count * ROWS, RADIX_B), BF16),
            pltpu.VMEM((128 * quads, 2 * RADIX_B), BF16),
            pltpu.VMEM((rows, 128), F32),
        ],
        compiler_params=pltpu.CompilerParams(vmem_limit_bytes=VMEM_LIMIT),
        cost_estimate=pl.CostEstimate(
            flops=2 * 2 * stations * count * LENGTH * (4 * 64 + 256 + 24),
            bytes_accessed=2 * x.size + 2 * rows * 128,
            transcendentals=0,
        ),
    )(*operands)


def weights_body(upper_ref, codes_ref, scale_ref, out_ref):
    upper = upper_ref[0]
    unit = 2.0 * np.pi / LENGTH

    def step(at, carry):
        row = pl.multiple_of(at // 8 * 16, 16)
        col = pl.multiple_of(at % 8 * 128, 128)
        codes = codes_ref[pl.ds(row, 16), pl.ds(col, 128)]
        scale = scale_ref[:, pl.ds(col, 128)]
        start = ((codes * (upper * RADIX_A)) & (LENGTH - 1)).astype(F32) * unit
        by = codes.astype(F32) * unit
        odd = (lax.broadcasted_iota(jnp.int32, (16, 128), 1) & 1) == 1
        cosine = jnp.cos(start) * scale
        sine = jnp.sin(start) * scale
        upper_row = jnp.where(odd, sine, cosine)
        lower_row = jnp.where(odd, cosine, -sine)
        by_cos = jnp.cos(by)
        by_sin = jnp.sin(by)
        for c1 in range(RADIX_A):
            out_ref[c1, pl.ds(row, 16), pl.ds(col, 128)] = upper_row.astype(BF16)
            out_ref[c1, pl.ds(row + 64, 16), pl.ds(col, 128)] = lower_row.astype(BF16)
            if c1 + 1 < RADIX_A:
                upper_row, lower_row = (
                    upper_row * by_cos + lower_row * by_sin,
                    lower_row * by_cos - upper_row * by_sin,
                )
        return carry

    lax.fori_loop(0, 32, step, 0)


def beam_weights(upper, codes, flags):
    stations = codes.shape[1]
    codes = jnp.repeat(codes, 2, axis=1)
    scale = flags.astype(F32) / jnp.sqrt(jnp.float32(stations))
    scale = jnp.repeat(scale, 2)[None, :]
    return pl.pallas_call(
        weights_body,
        out_shape=jax.ShapeDtypeStruct((RADIX_A, 128, 2 * stations), BF16),
        in_specs=[
            pl.BlockSpec(memory_space=pltpu.SMEM),
            pl.BlockSpec(memory_space=pltpu.VMEM),
            pl.BlockSpec(memory_space=pltpu.VMEM),
        ],
        out_specs=pl.BlockSpec(memory_space=pltpu.VMEM),
        compiler_params=pltpu.CompilerParams(vmem_limit_bytes=VMEM_LIMIT),
        cost_estimate=pl.CostEstimate(
            flops=8 * RADIX_A * 128 * 2 * stations,
            bytes_accessed=2 * RADIX_A * 128 * 2 * stations,
            transcendentals=0,
        ),
    )(upper, codes, scale)


def beams_body(quads, held, last, x_ref, w_ref, *refs):
    if last:
        early_ref, out_ref, total = refs
    else:
        out_ref, = refs
        total = None
    lane = lax.broadcasted_iota(jnp.int32, (1, 128), 1)
    for group in range(quads):
        low = group * 128 // (16 * quads)
        data = x_ref[:, group].reshape(8 * 128, 128)
        picked = None
        for c in range(held):
            got = jnp.dot(w_ref[4 * low + c], data, preferred_element_type=F32)
            where = group * 128 + lane
            c1 = where // (16 * quads) * 4 + where % 16 // 4
            picked = jnp.where(c1 == 4 * low + c, got, 0.0 if picked is None else picked)
        turned = picked.T
        for m in range(0, 128, 4):
            at = group * 128 + m
            c1 = at // (16 * quads) * 4 + at % 16 // 4
            q = at % (16 * quads) // 16
            pol = q // (quads // 2)
            t = q % (quads // 2) * QUAD
            piece = turned[m : m + 4]
            if last:
                total[c1, pol, t : t + QUAD, :] = piece
            else:
                out_ref[c1, pol, t : t + QUAD, :] = piece
    if last:
        spectra = total.shape[2]
        early = early_ref.shape[2]
        for c1 in range(RADIX_A):
            for pol in range(2):
                total[c1, pol, spectra - early :, :] = early_ref[c1, pol]
        out_ref[...] = total[...].astype(BF16)


def beams(received, weights, quads, early):
    count = quads * QUAD // 2
    held = 4 * max(
        (g * 128 + 127) // (16 * quads) - g * 128 // (16 * quads) + 1 for g in range(quads)
    )
    received = received.reshape(RADIX_B, quads, 8, 128)
    operands = [received, weights]
    last = early is not None
    scratch = []
    if last:
        operands.append(early)
        spectra = count + early.shape[2]
        out_shape = jax.ShapeDtypeStruct((RADIX_A, 2, spectra, 128), BF16)
        scratch = [pltpu.VMEM((RADIX_A, 2, spectra, 128), F32)]
    else:
        out_shape = jax.ShapeDtypeStruct((RADIX_A, 2, count, 128), F32)
    return pl.pallas_call(
        functools.partial(beams_body, quads, held, last),
        out_shape=out_shape,
        in_specs=[pl.BlockSpec(memory_space=pltpu.VMEM)] * len(operands),
        out_specs=pl.BlockSpec(memory_space=pltpu.VMEM),
        scratch_shapes=scratch,
        compiler_params=pltpu.CompilerParams(vmem_limit_bytes=VMEM_LIMIT),
        cost_estimate=pl.CostEstimate(
            flops=2 * quads * held * 128 * 1024 * 128,
            bytes_accessed=2 * weights.size + 2 * received.size,
            transcendentals=0,
        ),
    )(*operands)


def turn(spectra):
    spectra = spectra.reshape(RADIX_B, -1, 128)
    return lax.all_to_all(spectra, "stn", split_axis=0, concat_axis=0, tiled=True)


def shards(samples, taps, codes, flags):
    stations = samples.shape[0]
    frames = samples.shape[3] // LENGTH
    size = lax.axis_size("tm")
    x = samples.reshape(stations, 2, 2, frames * RADIX_A, RADIX_B)
    x = x.transpose(0, 1, 3, 2, 4).reshape(stations, 2, frames * ROWS, RADIX_B)
    history = x[:, :, (frames - TAPS + 1) * ROWS :]
    halo = lax.ppermute(history, "tm", [(i, i + 1) for i in range(size - 1)])

    tables = (jnp.asarray(outer_table()), jnp.asarray(twiddles()), jnp.asarray(inner_table()))
    late = frames - QUAD
    early_sent = channelise(x, None, taps, tables, late, QUAD)
    early_got = turn(early_sent)
    upper = lax.axis_index("stn").astype(jnp.int32).reshape(1)
    weights = beam_weights(upper, codes, flags)
    main_sent = channelise(x, halo, taps, tables, 0, late)
    main_got = turn(main_sent)
    early = beams(early_got, weights, 2, None)
    return beams(main_got, weights, 2 * late // QUAD, early)


def solution(mesh):
    in_specs = (P("stn", None, None, "tm"), P(), P(), P())
    out_specs = P("stn", None, "tm", None)
    return jax.shard_map(shards, mesh=mesh, in_specs=in_specs, out_specs=out_specs, check_vma=False)
```

time: 172 us -> 118 us (0.69)
  local copies, waits for them, and re-layouts: 56.7 us -> 4.74 us
  other arithmetic: 39.7 us -> 0.01 us
  Pallas kernels: 0 us -> 35.4 us
  matrix products: 14.8 us -> 0 us
  starting transfers between devices: 16.5 us -> 31.1 us
  waiting for transfers between devices: 43.3 us -> 46.3 us
    pallas_call x0 -> x5, Pallas kernels: none -> 35.4 us  [the longest x2 13.4 us: beams(): pl.pallas_call(functools.partial(beams_body, quads, held, last), out_shap...]
    unnamed x10 -> x17, local copies, waits for them, and re-layouts: 21.6 us -> 1.33 us
    reshape x4 -> x1, local copies, waits for them, and re-layouts: 20.1 us -> 0.18 us  [beam_weights(): codes = jnp.repeat(codes, 2, axis=1)]
    convert_element_type x3 -> x0, other arithmetic: 18.1 us -> none  [the longest x1 17.7 us: beam_weights(): (-jnp.sin(angles) * scale[None, None, :, None]).astype(jnp.bfloat16)]
    neg x3 -> x0, other arithmetic: 16.9 us -> none  [the longest x1 16.5 us: beam_weights(): second_row = jnp.stack([-imag_part, real_part], axis=3)]
    dot_general x3 -> x0, matrix products: 14.8 us -> none  [the longest x1 6.44 us: shards(): jnp.einsum('cspfoe,ecosrb->ecpfrb', turned, weights, preferred_element_ty...]
    all_to_all x1 -> x2, starting transfers between devices: 15.2 us -> 29.8 us  [turn(): lax.all_to_all(spectra, 'stn', split_axis=0, concat_axis=0, tiled=True)]
    all_to_all x1 -> x2, waiting for transfers between devices: 14 us -> 25.4 us  [turn(): lax.all_to_all(spectra, 'stn', split_axis=0, concat_axis=0, tiled=True)]
  transfers between devices with their start and end apart: 2 -> 3, of which waited for: 2 -> 2; matrix products, arithmetic and copies ran while one was open for 25% -> 1% of each run, Pallas kernels for 0% -> 24%
where the time goes in v1:
time: 118 us
  waiting for transfers between devices  46.3 us (39%)
  Pallas kernels  35.4 us (30%)
  starting transfers between devices  31.1 us (26%)
  local copies, waits for them, and re-layouts  4.74 us (4%)
    all_to_all x2, starting transfers between devices, turn(): lax.all_to_all(spectra, 'stn', split_axis=0, concat_axis=0, tiled=True)  29.8 us
    all_to_all x2, waiting for transfers between devices, turn(): lax.all_to_all(spectra, 'stn', split_axis=0, concat_axis=0, tiled=True)  25.4 us
    ppermute x1, waiting for transfers between devices, shards(): halo = lax.ppermute(history, 'tm', [(i, i + 1) for i in range(size - 1)])  20.9 us
    pallas_call x2, Pallas kernels, beams(): pl.pallas_call(functools.partial(beams_body, quads, held, last), out_shap...  13.4 us
    pallas_call x2, Pallas kernels, channelise(): pl.pallas_call(functools.partial(channelise_body, first, count, quads), g...  13.2 us
    pallas_call x1, Pallas kernels, beam_weights(): pl.pallas_call(weights_body, out_shape=jax.ShapeDtypeStruct((RADIX_A, 128...  8.85 us
    slice x1, local copies, waits for them, and re-layouts, shards(): history = x[:, :, (frames - TAPS + 1) * ROWS:]  2.74 us
  transfers between devices with their start and end apart: 3, of which 2 were waited for; matrix products, arithmetic and copies ran while one was open for 1% of the time, Pallas kernels for 24%

profile of v1, /device:TPU:7, one launch (start us, length us, event | category | flops | bytes accessed | tf_op | source)
XLA Modules:
  0.0 117.7 jit_solution(13124144772580434707)
XLA Ops:
  0.0 0.0 copy-start.3
  0.0 0.0 copy-start.4
  0.0 0.0 copy-start.5
  0.0 0.0 copy-start
  0.0 0.0 copy-start.2
  0.0 2.7 %slice.4 = bf16[4,2,704,128]{3,2,1,0:T(8,128)(2,1)} slice(bf16[4,2,1024,128]{3,2,1,0:T(8,128)(2,1)} %bitcast.11), slice={[0:4], [0:2], [320:1024], [0:128]} | slice | bytes 2883584 | tf_op jit(solution)/shard_map/slice | solution.py:310
  2.8 1.3 %collective-permute-start = (bf16[4,2,704,128]{3,2,1,0:T(8,128)(2,1)}, bf16[4,2,704,128]{3,2,1,0:T(8,128)(2,1)}, u32[]{:S(2)}, u32[]{:S(2)}) collective-permute-start(bf16[4,2,704,128]{3,2,1,0:T(8,128)(2,1)} %slice.4), channel_id=1, source_target_pairs={{0,1},{2,3},{4,5},{6,7},{8,9},{10,11},{12,13},{14,15},{16,17},{18,... | collective-permute-start | bytes 4325384 | tf_op jit(solution)/shard_map/ppermute | solution.py:311
  4.1 0.0 copy-done.3
  4.1 0.0 copy-done.4
  4.1 0.0 copy-done.5
  4.1 0.0 copy-done
  4.1 0.0 copy-done.2
  4.1 4.6 %shard_map.75 = bf16[2048,128]{1,0:T(8,128)(2,1)} custom-call(bf16[4,2,1024,128]{3,2,1,0:T(8,128)(2,1)S(1)} %bitcast.12, f32[12,4096]{1,0:T(8,128)S(1)} %copy-done.2, bf16[256,256]{1,0:T(8,128)(2,1)S(1)} %copy-done.5, f32[2,128,128]{2,1,0:T(8,128)S(1)} %copy-done.4, bf16[256,256]{1,0:T(8,128)(2,1)S(1)} %copy-done.3), custom_call_target="tpu_custom_call" | custom-call | flops 140509184 | bytes 2621440 | tf_op jit(solution)/shard_map/pallas_call | solution.py:156
  8.7 14.2 %all-to-all-start.1 = ((bf16[128,16,128]{2,1,0:T(8,128)(2,1)}), bf16[128,16,128]{2,1,0:T(8,128)(2,1)S(1)}, u32[]{:S(2)}, u32[]{:S(2)}) async-start(bf16[128,16,128]{2,1,0:T(8,128)(2,1)} %bitcast.9), calls=%async_computation.1 | async-start | bytes 1048576 | tf_op jit(solution)/shard_map/all_to_all | solution.py:301
  23.0 20.9 %collective-permute-done.refs_1_ = bf16[4,2,704,128]{3,2,1,0:T(8,128)(2,1)} collective-permute-done((bf16[4,2,704,128]{3,2,1,0:T(8,128)(2,1)}, bf16[4,2,704,128]{3,2,1,0:T(8,128)(2,1)}, u32[]{:S(2)}, u32[]{:S(2)}) %collective-permute-start) | collective-permute-done | bytes 1441824 | tf_op jit(solution)/shard_map/ppermute | solution.py:311
  43.8 8.5 %shard_map.73 = bf16[6144,128]{1,0:T(8,128)(2,1)S(1)} custom-call(bf16[4,2,1024,128]{3,2,1,0:T(8,128)(2,1)S(1)} %bitcast.13, bf16[4,2,704,128]{3,2,1,0:T(8,128)(2,1)} %collective-permute-done.refs_1_, f32[12,4096]{1,0:T(8,128)S(1)} %copy-done.2, bf16[256,256]{1,0:T(8,128)(2,1)S(1)} %copy-done.5, f32[2,128,128]{2,1,0:T(8,128)S(1)} %copy-done.4, ...), custom_call_target="tpu_custom_call" | custom-call | flops 421527552 | bytes 3670016 | tf_op jit(solution)/shard_map/pallas_call | solution.py:156
  52.4 0.0 copy-start.1
  52.4 1.2 copy-done.1
  53.6 0.0 all-to-all-done.1
  53.6 0.0 copy-start.7
  53.6 15.6 %all-to-all-start = ((bf16[128,48,128]{2,1,0:T(8,128)(2,1)}), bf16[128,48,128]{2,1,0:T(8,128)(2,1)S(1)}, u32[]{:S(2)}, u32[]{:S(2)}) async-start(bf16[128,48,128]{2,1,0:T(8,128)(2,1)} %bitcast.15), calls=%async_computation | async-start | bytes 3145728 | tf_op jit(solution)/shard_map/all_to_all | solution.py:301
  69.2 0.0 copy-done.7
  69.2 0.1 broadcast_in_dim.7
  69.3 0.2 broadcast_in_dim_reshape.3.scale_ref
  69.5 0.0 copy-done.6
  69.5 0.1 copy.10
  69.6 0.2 broadcast_in_dim.6
  69.8 0.2 copy.11.codes_ref
  70.0 8.8 %shard_map.74.w_ref = bf16[32,128,1024]{2,1,0:T(8,128)(2,1)} custom-call(s32[1]{0:T(128)} %bitcast.7.upper_ref, s32[64,1024]{1,0:T(8,128)S(1)} %copy.11.codes_ref, f32[1,1024]{1,0:T(1,128)S(1)} %broadcast_in_dim_reshape.3.scale_ref), custom_call_target="tpu_custom_call" | custom-call | flops 33554432 | bytes 8388608 | tf_op jit(solution)/shard_map/pallas_call | solution.py:213
  78.9 5.8 %shard_map.76.refs_0_ = f32[32,2,4,128]{3,2,1,0:T(4,128)S(1)} custom-call(bf16[128,2,8,128]{3,2,1,0:T(8,128)(2,1)S(1)} %bitcast.16, bf16[32,128,1024]{2,1,0:T(8,128)(2,1)} %shard_map.74.w_ref), custom_call_target="tpu_custom_call" | custom-call | flops 1073741824 | bytes 8912896 | tf_op jit(solution)/shard_map/pallas_call | solution.py:284
  84.6 25.4 %all-to-all-done = bf16[128,48,128]{2,1,0:T(8,128)(2,1)S(1)} async-done(((bf16[128,48,128]{2,1,0:T(8,128)(2,1)}), bf16[128,48,128]{2,1,0:T(8,128)(2,1)S(1)}, u32[]{:S(2)}, u32[]{:S(2)}) %all-to-all-start) | async-done | bytes 1572896 | tf_op jit(solution)/shard_map/all_to_all | solution.py:301
  110.0 7.6 %shard_map.77 = bf16[32,2,16,128]{3,2,1,0:T(8,128)(2,1)} custom-call(bf16[128,6,8,128]{3,2,1,0:T(8,128)(2,1)S(1)} %bitcast.14, bf16[32,128,1024]{2,1,0:T(8,128)(2,1)} %shard_map.74.w_ref, f32[32,2,4,128]{3,2,1,0:T(4,128)S(1)} %shard_map.76.refs_0_), custom_call_target="tpu_custom_call" | custom-call | flops 1610612736 | bytes 9961472 | tf_op jit(solution)/shard_map/pallas_call | solution.py:284
  (2 shorter events, 0.0 us)
Async XLA Ops:
  0.0 4.1 %copy-start.3 = (bf16[256,256]{1,0:T(8,128)(2,1)S(1)}, bf16[256,256]{1,0:T(8,128)(2,1)}, u32[]{:S(2)}) copy-start(bf16[256,256]{1,0:T(8,128)(2,1)} %constant.17.clone.refs_5_.refs_4_) | copy-start | bytes 393220
  0.0 4.1 %copy-start.4 = (f32[2,128,128]{2,1,0:T(8,128)S(1)}, f32[2,128,128]{2,1,0:T(8,128)}, u32[]{:S(2)}) copy-start(f32[2,128,128]{2,1,0:T(8,128)} %constant.16.clone.refs_4_.refs_3_) | copy-start | bytes 393220
  0.0 4.1 %copy-start.5 = (bf16[256,256]{1,0:T(8,128)(2,1)S(1)}, bf16[256,256]{1,0:T(8,128)(2,1)}, u32[]{:S(2)}) copy-start(bf16[256,256]{1,0:T(8,128)(2,1)} %constant.15.clone.refs_3_.refs_2_) | copy-start | bytes 393220
  0.0 4.1 %copy-start = (bf16[4,2,2,65536]{3,2,1,0:T(2,128)(2,1)S(1)}, bf16[4,2,2,65536]{3,2,1,0:T(2,128)(2,1)}, u32[]{:S(2)}) copy-start(bf16[4,2,2,65536]{3,2,1,0:T(2,128)(2,1)} %param.7) | copy-start | bytes 6291460
  0.0 4.1 %copy-start.2 = (f32[12,4096]{1,0:T(8,128)S(1)}, f32[12,4096]{1,0:T(8,128)}, u32[]{:S(2)}) copy-start(f32[12,4096]{1,0:T(8,128)} %refs_1_.1) | copy-start | bytes 589828
  2.8 41.1 %collective-permute-start = (bf16[4,2,704,128]{3,2,1,0:T(8,128)(2,1)}, bf16[4,2,704,128]{3,2,1,0:T(8,128)(2,1)}, u32[]{:S(2)}, u32[]{:S(2)}) collective-permute-start(bf16[4,2,704,128]{3,2,1,0:T(8,128)(2,1)} %slice.4), channel_id=1, source_target_pairs={{0,1},{2,3},{4,5},{6,7},{8,9},{10,11},{12,13},{14,15},{16,17},{18,... | collective-permute-start | bytes 4325384 | tf_op jit(solution)/shard_map/ppermute | solution.py:311
  8.7 44.8 %all-to-all-start.1 = ((bf16[128,16,128]{2,1,0:T(8,128)(2,1)}), bf16[128,16,128]{2,1,0:T(8,128)(2,1)S(1)}, u32[]{:S(2)}, u32[]{:S(2)}) async-start(bf16[128,16,128]{2,1,0:T(8,128)(2,1)} %bitcast.9), calls=%async_computation.1 | async-start | bytes 1048576 | tf_op jit(solution)/shard_map/all_to_all | solution.py:301
  52.4 1.2 %copy-start.1 = (bf16[6144,128]{1,0:T(8,128)(2,1)}, bf16[6144,128]{1,0:T(8,128)(2,1)S(1)}, u32[]{:S(2)}) copy-start(bf16[6144,128]{1,0:T(8,128)(2,1)S(1)} %shard_map.73) | copy-start | bytes 4718596
  53.6 15.6 %copy-start.7 = (s32[512]{0:T(512)S(1)}, s32[512]{0:T(512)}, u32[]{:S(2)}) copy-start(s32[512]{0:T(512)} %param.10) | copy-start | bytes 6148
  53.6 15.9 %copy-start.6 = (s32[64,512]{1,0:T(8,128)S(1)}, s32[64,512]{1,0:T(8,128)}, u32[]{:S(2)}) copy-start(s32[64,512]{1,0:T(8,128)} %param.9) | copy-start | bytes 393220
  53.6 56.4 %all-to-all-start = ((bf16[128,48,128]{2,1,0:T(8,128)(2,1)}), bf16[128,48,128]{2,1,0:T(8,128)(2,1)S(1)}, u32[]{:S(2)}, u32[]{:S(2)}) async-start(bf16[128,48,128]{2,1,0:T(8,128)(2,1)} %bitcast.15), calls=%async_computation | async-start | bytes 3145728 | tf_op jit(solution)/shard_map/all_to_all | solution.py:301

commit v2 on v1

v2 whole, which is shorter than its diff:
```python
import functools

import jax
import jax.numpy as jnp
import ml_dtypes
import numpy as np
from jax import lax
from jax.experimental import pallas as pl
from jax.experimental.pallas import tpu as pltpu
from jax.sharding import PartitionSpec as P

RADIX_A = 32
RADIX_B = 128
TAPS = 12
LENGTH = RADIX_A * RADIX_B
ROWS = 2 * RADIX_A
QUAD = 4
BF16 = jnp.bfloat16
F32 = jnp.float32
VMEM_LIMIT = 20 << 20


def params():
    return pltpu.CompilerParams(vmem_limit_bytes=VMEM_LIMIT)


def in_hbm(array):
    return pltpu.with_memory_space_constraint(array, pltpu.HBM)


IN_VMEM = pl.BlockSpec(memory_space=pltpu.VMEM)
IN_HBM = pl.BlockSpec(memory_space=pltpu.HBM)
LIGHT = pl.CostEstimate(flops=1024, bytes_accessed=1024, transcendentals=0)


def dft_table(radix):
    indices = np.arange(radix)
    angles = (indices[:, None] * indices[None, :] % radix) * (2.0 * np.pi / radix)
    cosine = np.cos(angles).astype(ml_dtypes.bfloat16)
    sine = np.sin(angles).astype(ml_dtypes.bfloat16)
    return np.stack(
        [np.stack([cosine, -sine], axis=1), np.stack([sine, cosine], axis=1)], axis=0
    )


def outer_table():
    table = dft_table(RADIX_A)
    grid = np.zeros((2, RADIX_A, QUAD, QUAD, RADIX_A, 2), ml_dtypes.bfloat16)
    for i in range(QUAD):
        grid[:, :, i, i] = table.transpose(2, 3, 1, 0)
    return grid.reshape(2 * RADIX_A * QUAD, QUAD * ROWS)


def inner_table():
    return dft_table(RADIX_B).reshape(2 * RADIX_B, 2 * RADIX_B).T.copy()


def twiddles():
    c1 = np.repeat(np.arange(RADIX_A), QUAD)
    angles = (c1[:, None] * np.arange(RADIX_B)[None, :] % LENGTH) * (2.0 * np.pi / LENGTH)
    scale = 1.0 / np.sqrt(np.float64(LENGTH))
    return np.stack([np.cos(angles) * scale, np.sin(angles) * scale]).astype(np.float32)


def spread_taps(taps_ref, taps2):
    for a in range(RADIX_A):
        for k in range(TAPS):
            row = taps_ref[k : k + 1, a * RADIX_B : (a + 1) * RADIX_B]
            taps2[k, 2 * a : 2 * a + 2, :] = jnp.broadcast_to(row, (2, RADIX_B))


def fir(first, count, base, stations, x_ref, halo_ref, taps2, filt):
    pieces = ROWS // 16

    def step(at, carry):
        station = at // (2 * pieces)
        pol = at // pieces % 2
        row = pl.multiple_of(at % pieces * 16, 16)
        frames = []
        for f in range(first - TAPS + 1, first + count):
            if f < 0:
                where = pl.multiple_of((f + TAPS - 1) * ROWS + row, 16)
                piece = halo_ref[station, pol, pl.ds(where, 16), :]
            else:
                where = pl.multiple_of(f * ROWS + row, 16)
                piece = x_ref[base + station, pol, pl.ds(where, 16), :]
            frames.append(piece.astype(F32))
        taps = [taps2[k, pl.ds(row, 16), :] for k in range(TAPS)]
        halves = []
        for half in range(2):
            rows = slice(8 * half, 8 * half + 8)
            outs = []
            for t in range(count):
                total = taps[0][rows] * frames[t][rows]
                for k in range(1, TAPS):
                    total = total + taps[k][rows] * frames[t + k][rows]
                outs.append(total)
            halves.append(outs)
        for t in range(count):
            both = jnp.concatenate([halves[0][t], halves[1][t]], axis=0).astype(BF16)
            where = pl.multiple_of(((station * 2 + pol) * count + t) * ROWS + row, 16)
            filt[pl.ds(where, 16), :] = both
        return carry

    lax.fori_loop(0, stations * 2 * pieces, step, 0)


def outer_stage(quads, stations, base, filt, outer_ref, tw_ref, mid):
    half = RADIX_A * QUAD
    size = QUAD * ROWS
    cosine = tw_ref[0]
    sine = tw_ref[1]
    table = outer_ref[...]
    for s in range(stations):
        for pair in range(quads // 2):
            at = (s * quads + 2 * pair) * size
            data = jnp.concatenate([filt[at : at + size, :], filt[at + size : at + 2 * size, :]], axis=1)
            got = jnp.dot(table, data, preferred_element_type=F32)
            for side in range(2):
                q = 2 * pair + side
                real = got[:half, side * 128 : side * 128 + 128]
                imag = got[half:, side * 128 : side * 128 + 128]
                real_out = (real * cosine + imag * sine).astype(BF16)
                imag_out = (imag * cosine - real * sine).astype(BF16)
                for g in range(half // 16):
                    to = ((base + s) * half // 16 * quads + g * quads + q) * 16
                    mid[to : to + 16, :RADIX_B] = real_out[16 * g : 16 * g + 16]
                    mid[to : to + 16, RADIX_B:] = imag_out[16 * g : 16 * g + 16]


def inner_stage(quads, station, data_ref, start, inner_ref, turn):
    block = 8 * quads
    for pair in range(quads // 2):
        at = start + pair * 256
        got = lax.dot_general(
            inner_ref[...],
            data_ref[at : at + 256, :],
            (((1,), (1,)), ((), ())),
            preferred_element_type=F32,
        )
        for side in range(2):
            group = 2 * pair + side
            for part in range(2):
                for c in range(0, RADIX_B, 8):
                    to = c * block + group * 8 + part + 2 * station
                    turn[pl.ds(to, 8, stride=block), :] = got[
                        part * RADIX_B + c : part * RADIX_B + c + 8,
                        side * 128 : side * 128 + 128,
                    ]


def send_out(turn, packed, out_ref, sems):
    rows = turn.shape[0]
    parts = sems.shape[0]
    size = rows // parts
    copies = []
    for p in range(parts):
        packed[p * size : (p + 1) * size, :] = turn[p * size : (p + 1) * size, :].astype(BF16)
        copy = pltpu.make_async_copy(
            packed.at[pl.ds(p * size, size)], out_ref.at[pl.ds(p * size, size)], sems.at[p]
        )
        copy.start()
        copies.append(copy)
    for copy in copies:
        copy.wait()


def early_body(
    first, count, quads, stations, x_hbm, taps_hbm, outer_hbm, tw_hbm, inner_hbm,
    out_ref, taps2, x_ref, taps_ref, outer_ref, tw_ref, inner_ref, filt, mid, turn, packed, sems, in_sems,
):
    pairs = [(taps_hbm, taps_ref)]
    pairs += [(x_hbm.at[s], x_ref.at[s]) for s in range(stations)]
    pairs += [(outer_hbm, outer_ref), (tw_hbm, tw_ref), (inner_hbm, inner_ref)]
    copies = [pltpu.make_async_copy(a, b, in_sems.at[i]) for i, (a, b) in enumerate(pairs)]
    for copy in copies:
        copy.start()
    copies[0].wait()
    spread_taps(taps_ref, taps2)
    for s in range(stations):
        copies[1 + s].wait()
    fir(first, count, 0, stations, x_ref, None, taps2, filt)
    for copy in copies[1 + stations :]:
        copy.wait()
    outer_stage(quads, stations, 0, filt, outer_ref, tw_ref, mid)
    for s in range(stations):
        inner_stage(quads, s, mid, s * 128 * quads, inner_ref, turn)
    send_out(turn, packed, out_ref, sems)


def half_body(count, quads, stations, x_ref, halo_ref, taps2, outer_ref, tw_ref, mid_ref, filt):
    fir(0, count, 0, stations, x_ref, halo_ref, taps2, filt)
    outer_stage(quads, stations, 0, filt, outer_ref, tw_ref, mid_ref)


def rest_body(
    count, quads, base, stations, x_ref, halo_ref, taps2, outer_ref, tw_ref, inner_ref, before_ref,
    out_ref, filt, mid, turn, packed, sems,
):
    fir(0, count, base, stations, x_ref, halo_ref, taps2, filt)
    for s in range(base):
        inner_stage(quads, s, before_ref, s * 128 * quads, inner_ref, turn)
    outer_stage(quads, stations, 0, filt, outer_ref, tw_ref, mid)
    for s in range(stations):
        inner_stage(quads, base + s, mid, s * 128 * quads, inner_ref, turn)
    send_out(turn, packed, out_ref, sems)


def channelise_early(x, taps, outer, tw, inner, first, count):
    stations = x.shape[0]
    quads = 2 * count // QUAD
    rows = RADIX_B * 8 * quads
    return pl.pallas_call(
        functools.partial(early_body, first, count, quads, stations),
        out_shape=(
            pltpu.HBM((rows, 128), BF16),
            jax.ShapeDtypeStruct((TAPS, ROWS, RADIX_B), F32),
        ),
        in_specs=[IN_HBM] * 5,
        out_specs=(IN_HBM, IN_VMEM),
        scratch_shapes=[
            pltpu.VMEM(x.shape, BF16),
            pltpu.VMEM(taps.shape, F32),
            pltpu.VMEM(outer.shape, BF16),
            pltpu.VMEM(tw.shape, F32),
            pltpu.VMEM(inner.shape, BF16),
            pltpu.VMEM((stations * 2 * count * ROWS, RADIX_B), BF16),
            pltpu.VMEM((stations * 128 * quads, 2 * RADIX_B), BF16),
            pltpu.VMEM((rows, 128), F32),
            pltpu.VMEM((rows, 128), BF16),
            pltpu.SemaphoreType.DMA((4,)),
            pltpu.SemaphoreType.DMA((stations + 4,)),
        ],
        compiler_params=params(),
        cost_estimate=LIGHT,
    )(*map(in_hbm, (x, taps, outer, tw, inner)))


def channelise_half(x, halo, taps2, outer, tw, count):
    stations = halo.shape[0]
    quads = 2 * count // QUAD
    return pl.pallas_call(
        functools.partial(half_body, count, quads, stations),
        out_shape=jax.ShapeDtypeStruct((stations * 128 * quads, 2 * RADIX_B), BF16),
        in_specs=[IN_VMEM] * 5,
        out_specs=IN_VMEM,
        scratch_shapes=[pltpu.VMEM((stations * 2 * count * ROWS, RADIX_B), BF16)],
        compiler_params=params(),
        cost_estimate=LIGHT,
    )(x, halo, taps2, outer, tw)


def channelise_rest(x, halo, taps2, outer, tw, inner, before, count):
    stations = halo.shape[0]
    base = x.shape[0] - stations
    quads = 2 * count // QUAD
    rows = RADIX_B * 8 * quads
    return pl.pallas_call(
        functools.partial(rest_body, count, quads, base, stations),
        out_shape=pltpu.HBM((rows, 128), BF16),
        in_specs=[IN_VMEM] * 7,
        out_specs=IN_HBM,
        scratch_shapes=[
            pltpu.VMEM((stations * 2 * count * ROWS, RADIX_B), BF16),
            pltpu.VMEM((stations * 128 * quads, 2 * RADIX_B), BF16),
            pltpu.VMEM((rows, 128), F32),
            pltpu.VMEM((rows, 128), BF16),
            pltpu.SemaphoreType.DMA((8,)),
        ],
        compiler_params=params(),
        cost_estimate=LIGHT,
    )(x, halo, taps2, outer, tw, inner, before)


def history_body(station, start, x_ref, out_ref, sems):
    copies = []
    for s in range(out_ref.shape[0]):
        for pol in range(2):
            copy = pltpu.make_async_copy(
                x_ref.at[station + s, pol, pl.ds(start, out_ref.shape[2])],
                out_ref.at[s, pol],
                sems.at[2 * s + pol],
            )
            copy.start()
            copies.append(copy)
    for copy in copies:
        copy.wait()


def history(x, frames, station, stations):
    rows = frames * ROWS
    return pl.pallas_call(
        functools.partial(history_body, station, x.shape[2] - rows),
        out_shape=pltpu.VMEM((stations, 2, rows, RADIX_B), BF16),
        in_specs=[IN_HBM],
        out_specs=IN_VMEM,
        scratch_shapes=[pltpu.SemaphoreType.DMA((2 * stations,))],
        compiler_params=params(),
        cost_estimate=LIGHT,
    )(in_hbm(x))


def weights_body(upper_ref, codes_ref, scale_ref, hbm_ref, out_ref, sem):
    upper = upper_ref[0]
    unit = 2.0 * np.pi / LENGTH

    def step(at, carry):
        row = pl.multiple_of(at // 8 * 16, 16)
        col = pl.multiple_of(at % 8 * 128, 128)
        codes = codes_ref[pl.ds(row, 16), pl.ds(col, 128)]
        scale = scale_ref[:, pl.ds(col, 128)]
        start = ((codes * (upper * RADIX_A)) & (LENGTH - 1)).astype(F32) * unit
        by = codes.astype(F32) * unit
        odd = (lax.broadcasted_iota(jnp.int32, (16, 128), 1) & 1) == 1
        cosine = jnp.cos(start) * scale
        sine = jnp.sin(start) * scale
        here = jnp.where(odd, sine, cosine)
        across = jnp.where(odd, cosine, -sine)
        by_cos = jnp.cos(by)
        by_sin = jnp.sin(by)
        for c1 in range(RADIX_A):
            out_ref[c1, pl.ds(row, 16), pl.ds(col, 128)] = here.astype(BF16)
            if c1 + 1 < RADIX_A:
                here, across = here * by_cos + across * by_sin, across * by_cos - here * by_sin
        return carry

    lax.fori_loop(0, 32, step, 0)
    copy = pltpu.make_async_copy(out_ref, hbm_ref, sem)
    copy.start()
    copy.wait()


def beam_weights(upper, codes, flags):
    beam_count, stations = codes.shape
    codes = jnp.repeat(codes, 2, axis=1)
    scale = flags.astype(F32) / jnp.sqrt(jnp.float32(stations))
    scale = jnp.repeat(scale, 2)[None, :]
    shape = (RADIX_A, beam_count, 2 * stations)
    return pl.pallas_call(
        weights_body,
        out_shape=pltpu.HBM(shape, BF16),
        in_specs=[pl.BlockSpec(memory_space=pltpu.SMEM), IN_VMEM, IN_VMEM],
        out_specs=IN_HBM,
        scratch_shapes=[pltpu.VMEM(shape, BF16), pltpu.SemaphoreType.DMA],
        compiler_params=params(),
        cost_estimate=LIGHT,
    )(upper, codes, scale)


def beams_body(quads, last, x_ref, w_hbm, *refs):
    if last:
        early_ref, out_ref, total, w_ref, sems = refs
    else:
        out_ref, w_ref, sems = refs
        total = out_ref
    copies = []
    for g in range(RADIX_A // 4):
        part = pl.ds(4 * g, 4)
        copies.append(pltpu.make_async_copy(w_hbm.at[part], w_ref.at[part], sems.at[g]))
        copies[g].start()
    waited = 0
    beam_count = w_ref.shape[1]
    lane = lax.broadcasted_iota(jnp.int32, (1, 128), 1)
    even = (lax.broadcasted_iota(jnp.int32, (1, 8, 128), 1) & 1) == 0
    for group in range(quads):
        base = group * 128
        low = base // (16 * quads)
        high = (base + 127) // (16 * quads)
        values = x_ref[:, group]
        wide = values.astype(F32)
        swapped = jnp.where(even, pltpu.roll(wide, 7, 1), -pltpu.roll(wide, 1, 1)).astype(BF16)
        data = jnp.concatenate([values.reshape(1024, 128), swapped.reshape(1024, 128)], axis=1)
        c1 = (base + lane) // (16 * quads) * 4 + lane % 16 // 4
        real = imag = None
        for g in range(low, high + 1):
            while waited <= g:
                copies[waited].wait()
                waited += 1
            weights = w_ref[4 * g : 4 * g + 4].reshape(4 * beam_count, 1024)
            got = jnp.dot(weights, data, preferred_element_type=F32)
            for c in range(4):
                piece = got[beam_count * c : beam_count * (c + 1)]
                if real is None:
                    real, imag = piece[:, :128], piece[:, 128:]
                else:
                    mine = c1 == 4 * g + c
                    real = jnp.where(mine, piece[:, :128], real)
                    imag = jnp.where(mine, piece[:, 128:], imag)
        turned = jnp.concatenate([real, imag], axis=0).T
        for m in range(0, 128, 4):
            at = base + m
            channel = at // (16 * quads) * 4 + at % 16 // 4
            q = at % (16 * quads) // 16
            pol = q // (quads // 2)
            t = q % (quads // 2) * QUAD
            total[channel, pol, t : t + QUAD, :] = turned[m : m + 4]
    if last:
        spectra = total.shape[2]
        early = early_ref.shape[2]
        for channel in range(RADIX_A):
            for pol in range(2):
                total[channel, pol, spectra - early :, :] = early_ref[channel, pol]
        out_ref[...] = total[...].astype(BF16)


def beams(received, weights, quads, early):
    count = quads * QUAD // 2
    received = received.reshape(RADIX_B, quads, 8, 128)
    operands = [received, in_hbm(weights)]
    in_specs = [IN_VMEM, IN_HBM]
    scratch = [pltpu.VMEM(weights.shape, BF16), pltpu.SemaphoreType.DMA((RADIX_A // 4,))]
    last = early is not None
    if last:
        operands.append(early)
        in_specs.append(IN_VMEM)
        shape = (RADIX_A, 2, count + early.shape[2], 128)
        out_shape = jax.ShapeDtypeStruct(shape, BF16)
        scratch = [pltpu.VMEM(shape, F32)] + scratch
    else:
        out_shape = jax.ShapeDtypeStruct((RADIX_A, 2, count, 128), F32)
    return pl.pallas_call(
        functools.partial(beams_body, quads, last),
        out_shape=out_shape,
        in_specs=in_specs,
        out_specs=IN_VMEM,
        scratch_shapes=scratch,
        compiler_params=params(),
        cost_estimate=LIGHT,
    )(*operands)


def turn(spectra):
    spectra = spectra.reshape(RADIX_B, -1, 128)
    return lax.all_to_all(spectra, "stn", split_axis=0, concat_axis=0, tiled=True)


def shards(samples, taps, codes, flags):
    stations = samples.shape[0]
    frames = samples.shape[3] // LENGTH
    size = lax.axis_size("tm")
    x = samples.reshape(stations, 2, 2, frames * RADIX_A, RADIX_B)
    x = x.transpose(0, 1, 3, 2, 4).reshape(stations, 2, frames * ROWS, RADIX_B)
    pairs = [(i, i + 1) for i in range(size - 1)]
    halos = [
        lax.ppermute(history(x, TAPS - 1, station, count), "tm", pairs)
        for station, count in ((0, stations - 1), (stations - 1, 1))
    ]

    outer, tw, inner = jnp.asarray(outer_table()), jnp.asarray(twiddles()), jnp.asarray(inner_table())
    late = frames - QUAD
    early_sent, taps2 = channelise_early(x, taps, outer, tw, inner, late, QUAD)
    early_got = turn(early_sent)
    upper = lax.axis_index("stn").astype(jnp.int32).reshape(1)
    weights = beam_weights(upper, codes, flags)
    before = channelise_half(x, halos[0], taps2, outer, tw, late)
    main_sent = channelise_rest(x, halos[1], taps2, outer, tw, inner, before, late)
    main_got = turn(main_sent)
    early = beams(early_got, weights, 2, None)
    return beams(main_got, weights, 2 * late // QUAD, early)


def solution(mesh):
    in_specs = (P("stn", None, None, "tm"), P(), P(), P())
    out_specs = P("stn", None, "tm", None)
    return jax.shard_map(shards, mesh=mesh, in_specs=in_specs, out_specs=out_specs, check_vma=False)
```

time: 118 us -> 111 us (0.941)
  waiting for transfers between devices: 46.3 us -> 41.4 us
  local copies, waits for them, and re-layouts: 4.74 us -> 0.83 us
    ppermute x1 -> x2, waiting for transfers between devices: 20.9 us -> 13.4 us  [shards(): lax.ppermute(history(x, TAPS - 1, station, count), 'tm', pairs)]
    slice x1 -> x0, local copies, waits for them, and re-layouts: 2.74 us -> none  [shards(): history = x[:, :, (frames - TAPS + 1) * ROWS:]]
    all_to_all x2, waiting for transfers between devices: 25.4 us -> 27.9 us  [turn(): lax.all_to_all(spectra, 'stn', split_axis=0, concat_axis=0, tiled=True)]
    ppermute x1 -> x2, starting transfers between devices: 1.28 us -> 2.58 us  [shards(): lax.ppermute(history(x, TAPS - 1, station, count), 'tm', pairs)]
    pallas_call x5 -> x8, Pallas kernels: 35.4 us -> 35.4 us  [the longest x2 10.8 us: beams(): pl.pallas_call(functools.partial(beams_body, quads, last), out_shape=out_...]
  transfers between devices with their start and end apart: 3 -> 4, of which waited for: 2 -> 3; matrix products, arithmetic and copies ran while one was open for 1% -> 1% of each run, Pallas kernels for 24% -> 25%
where the time goes in v2:
time: 111 us; the launch traced here: 110 us
  waiting for transfers between devices  41.4 us (37%)
  Pallas kernels  35.4 us (32%)
  starting transfers between devices  32.2 us (29%)
    all_to_all x2, starting transfers between devices, turn(): lax.all_to_all(spectra, 'stn', split_axis=0, concat_axis=0, tiled=True)  29.6 us
    all_to_all x2, waiting for transfers between devices, turn(): lax.all_to_all(spectra, 'stn', split_axis=0, concat_axis=0, tiled=True)  27.9 us
    ppermute x2, waiting for transfers between devices, shards(): lax.ppermute(history(x, TAPS - 1, station, count), 'tm', pairs)  13.4 us
    pallas_call x2, Pallas kernels, beams(): pl.pallas_call(functools.partial(beams_body, quads, last), out_shape=out_...  10.8 us
    pallas_call x1, Pallas kernels, beam_weights(): pl.pallas_call(weights_body, out_shape=pltpu.HBM(shape, BF16), in_specs=[...  7.22 us
    pallas_call x1, Pallas kernels, channelise_early(): pl.pallas_call(functools.partial(early_body, first, count, quads, station...  5.19 us
    pallas_call x1, Pallas kernels, channelise_half(): pl.pallas_call(functools.partial(half_body, count, quads, stations), out_...  4.98 us
    pallas_call x1, Pallas kernels, channelise_rest(): pl.pallas_call(functools.partial(rest_body, count, quads, base, stations)...  3.83 us
  transfers between devices with their start and end apart: 4, of which 3 were waited for; matrix products, arithmetic and copies ran while one was open for 1% of the time, Pallas kernels for 25%

profile of v2, /device:TPU:7, one launch (start us, length us, event | category | flops | bytes accessed | tf_op | source)
XLA Modules:
  0.0 110.2 jit_solution(12269944244099412742)
XLA Ops:
  0.0 2.3 %shard_map.75 = bf16[3,2,704,128]{3,2,1,0:T(8,128)(2,1)} custom-call(bf16[4,2,1024,128]{3,2,1,0:T(8,128)(2,1)} %bitcast.11), custom_call_target="tpu_custom_call" | custom-call | flops 1024 | bytes 1024 | tf_op jit(solution)/shard_map/pallas_call | solution.py:292
  2.3 1.3 %collective-permute-start.1 = (bf16[3,2,704,128]{3,2,1,0:T(8,128)(2,1)}, bf16[3,2,704,128]{3,2,1,0:T(8,128)(2,1)}, u32[]{:S(2)}, u32[]{:S(2)}) collective-permute-start(bf16[3,2,704,128]{3,2,1,0:T(8,128)(2,1)} %shard_map.75), channel_id=1, source_target_pairs={{0,1},{2,3},{4,5},{6,7},{8,9},{10,11},{12,13},{14,15},{16,17},{18,... | collective-permute-start | bytes 3244040 | tf_op jit(solution)/shard_map/ppermute | solution.py:445
  3.6 5.2 %shard_map.74 = (bf16[2048,128]{1,0:T(8,128)(2,1)}, f32[12,64,128]{2,1,0:T(8,128)S(1)}) custom-call(bf16[4,2,1024,128]{3,2,1,0:T(8,128)(2,1)} %bitcast.12, f32[12,4096]{1,0:T(8,128)} %taps_hbm.1, bf16[256,256]{1,0:T(8,128)(2,1)} %constant.15.clone.outer_hbm.outer_ref, f32[2,128,128]{2,1,0:T(8,128)} %constant.16.clone.tw_hbm.tw_ref, ...), custom_call_target="tpu_custom_call" | custom-call | flops 1024 | bytes 1024 | tf_op jit(solution)/shard_map/pallas_call | solution.py:213
  8.8 0.0 copy-start
  8.9 0.0 copy-start.1
  8.9 0.0 copy-start.2
  8.9 14.4 %all-to-all-start.1 = ((bf16[128,16,128]{2,1,0:T(8,128)(2,1)}), bf16[128,16,128]{2,1,0:T(8,128)(2,1)S(1)}, u32[]{:S(2)}, u32[]{:S(2)}) async-start(bf16[128,16,128]{2,1,0:T(8,128)(2,1)} %bitcast.20), calls=%async_computation.1 | async-start | bytes 1048576 | tf_op jit(solution)/shard_map/all_to_all | solution.py:434
  23.2 1.0 shard_map.73
  24.3 1.3 %collective-permute-start = (bf16[1,2,704,128]{3,2,1,0:T(8,128)(2,1)S(1)}, bf16[1,2,704,128]{3,2,1,0:T(8,128)(2,1)S(1)}, u32[]{:S(2)}, u32[]{:S(2)}) collective-permute-start(bf16[1,2,704,128]{3,2,1,0:T(8,128)(2,1)S(1)} %shard_map.73), channel_id=1, source_target_pairs={{0,1},{2,3},{4,5},{6,7},{8,9},{10,11},{12,13},{14,15},{16,17},{18,... | collective-permute-start | bytes 1081352 | tf_op jit(solution)/shard_map/ppermute | solution.py:445
  25.6 5.5 %collective-permute-done.1.halo_ref = bf16[3,2,704,128]{3,2,1,0:T(8,128)(2,1)} collective-permute-done((bf16[3,2,704,128]{3,2,1,0:T(8,128)(2,1)}, bf16[3,2,704,128]{3,2,1,0:T(8,128)(2,1)}, u32[]{:S(2)}, u32[]{:S(2)}) %collective-permute-start.1) | collective-permute-done | bytes 1081376 | tf_op jit(solution)/shard_map/ppermute | solution.py:445
  31.1 0.0 copy-done
  31.1 0.0 copy-done.1
  31.1 0.0 copy-done.2
  31.1 0.0 copy-start.3
  31.1 5.0 %shard_map.76.before_ref = bf16[2304,256]{1,0:T(8,128)(2,1)S(1)} custom-call(bf16[4,2,1024,128]{3,2,1,0:T(8,128)(2,1)S(1)} %bitcast.14, bf16[3,2,704,128]{3,2,1,0:T(8,128)(2,1)} %collective-permute-done.1.halo_ref, f32[12,64,128]{2,1,0:T(8,128)S(1)} %get-tuple-element.7.taps2, bf16[256,256]{1,0:T(8,128)(2,1)S(1)} %copy-done.2, f32[2,128,128]{2,1,0:T(8,128)S(1)} %copy-done.1), custom_call_target="tpu_custom_call" | custom-call | flops 1024 | bytes 1024 | tf_op jit(solution)/shard_map/pallas_call | solution.py:242
  36.1 7.9 %collective-permute-done.halo_ref = bf16[1,2,704,128]{3,2,1,0:T(8,128)(2,1)S(1)} collective-permute-done((bf16[1,2,704,128]{3,2,1,0:T(8,128)(2,1)S(1)}, bf16[1,2,704,128]{3,2,1,0:T(8,128)(2,1)S(1)}, u32[]{:S(2)}, u32[]{:S(2)}) %collective-permute-start) | collective-permute-done | bytes 360480 | tf_op jit(solution)/shard_map/ppermute | solution.py:445
  44.0 0.0 copy-done.3
  44.0 3.8 %shard_map.77 = bf16[6144,128]{1,0:T(8,128)(2,1)} custom-call(bf16[4,2,1024,128]{3,2,1,0:T(8,128)(2,1)S(1)} %bitcast.15, bf16[1,2,704,128]{3,2,1,0:T(8,128)(2,1)S(1)} %collective-permute-done.halo_ref, f32[12,64,128]{2,1,0:T(8,128)S(1)} %get-tuple-element.7.taps2, bf16[256,256]{1,0:T(8,128)(2,1)S(1)} %copy-done.2, f32[2,128,128]{2,1,0:T(8,128)S(1)} %copy-done.1, ...), custom_call_target="tpu_custom_call" | custom-call | flops 1024 | bytes 1024 | tf_op jit(solution)/shard_map/pallas_call | solution.py:258
  47.9 0.0 all-to-all-done.1
  47.9 0.0 copy-start.5
  47.9 0.0 copy-start.4
  47.9 15.2 %all-to-all-start = ((bf16[128,48,128]{2,1,0:T(8,128)(2,1)}), bf16[128,48,128]{2,1,0:T(8,128)(2,1)S(1)}, u32[]{:S(2)}, u32[]{:S(2)}) async-start(bf16[128,48,128]{2,1,0:T(8,128)(2,1)} %bitcast.18), calls=%async_computation | async-start | bytes 3145728 | tf_op jit(solution)/shard_map/all_to_all | solution.py:434
  63.2 0.0 copy-done.5
  63.2 0.1 broadcast_in_dim.7
  63.3 0.2 broadcast_in_dim_reshape.3.scale_ref
  63.5 0.1 copy.10
  63.6 0.2 broadcast_in_dim.6
  63.8 0.2 copy.11.codes_ref
  64.0 7.2 %shard_map.78.w_hbm = bf16[32,64,1024]{2,1,0:T(8,128)(2,1)} custom-call(s32[1]{0:T(128)} %bitcast.7.upper_ref, s32[64,1024]{1,0:T(8,128)S(1)} %copy.11.codes_ref, f32[1,1024]{1,0:T(1,128)S(1)} %broadcast_in_dim_reshape.3.scale_ref), custom_call_target="tpu_custom_call" | custom-call | flops 1024 | bytes 1024 | tf_op jit(solution)/shard_map/pallas_call | solution.py:339
  71.2 4.8 %shard_map.79.refs_0_ = f32[32,2,4,128]{3,2,1,0:T(4,128)S(1)} custom-call(bf16[128,2,8,128]{3,2,1,0:T(8,128)(2,1)S(1)} %bitcast.17, bf16[32,64,1024]{2,1,0:T(8,128)(2,1)} %shard_map.78.w_hbm), custom_call_target="tpu_custom_call" | custom-call | flops 1024 | bytes 1024 | tf_op jit(solution)/shard_map/pallas_call | solution.py:421
  76.1 27.9 %all-to-all-done = bf16[128,48,128]{2,1,0:T(8,128)(2,1)S(1)} async-done(((bf16[128,48,128]{2,1,0:T(8,128)(2,1)}), bf16[128,48,128]{2,1,0:T(8,128)(2,1)S(1)}, u32[]{:S(2)}, u32[]{:S(2)}) %all-to-all-start) | async-done | bytes 1572896 | tf_op jit(solution)/shard_map/all_to_all | solution.py:434
  104.0 6.0 %shard_map.80 = bf16[32,2,16,128]{3,2,1,0:T(8,128)(2,1)} custom-call(bf16[128,6,8,128]{3,2,1,0:T(8,128)(2,1)S(1)} %bitcast.16, bf16[32,64,1024]{2,1,0:T(8,128)(2,1)} %shard_map.78.w_hbm, f32[32,2,4,128]{3,2,1,0:T(4,128)S(1)} %shard_map.79.refs_0_), custom_call_target="tpu_custom_call" | custom-call | flops 1024 | bytes 1024 | tf_op jit(solution)/shard_map/pallas_call | solution.py:421
  (2 shorter events, 0.0 us)
Async XLA Ops:
  2.3 28.8 %collective-permute-start.1 = (bf16[3,2,704,128]{3,2,1,0:T(8,128)(2,1)}, bf16[3,2,704,128]{3,2,1,0:T(8,128)(2,1)}, u32[]{:S(2)}, u32[]{:S(2)}) collective-permute-start(bf16[3,2,704,128]{3,2,1,0:T(8,128)(2,1)} %shard_map.75), channel_id=1, source_target_pairs={{0,1},{2,3},{4,5},{6,7},{8,9},{10,11},{12,13},{14,15},{16,17},{18,... | collective-permute-start | bytes 3244040 | tf_op jit(solution)/shard_map/ppermute | solution.py:445
  8.8 22.3 %copy-start = (bf16[4,2,2,65536]{3,2,1,0:T(2,128)(2,1)S(1)}, bf16[4,2,2,65536]{3,2,1,0:T(2,128)(2,1)}, u32[]{:S(2)}) copy-start(bf16[4,2,2,65536]{3,2,1,0:T(2,128)(2,1)} %param.7) | copy-start | bytes 6291460
  8.9 22.3 %copy-start.1 = (f32[2,128,128]{2,1,0:T(8,128)S(1)}, f32[2,128,128]{2,1,0:T(8,128)}, u32[]{:S(2)}) copy-start(f32[2,128,128]{2,1,0:T(8,128)} %constant.16.clone.tw_hbm.tw_ref) | copy-start | bytes 393220
  8.9 22.3 %copy-start.2 = (bf16[256,256]{1,0:T(8,128)(2,1)S(1)}, bf16[256,256]{1,0:T(8,128)(2,1)}, u32[]{:S(2)}) copy-start(bf16[256,256]{1,0:T(8,128)(2,1)} %constant.15.clone.outer_hbm.outer_ref) | copy-start | bytes 393220
  8.9 39.0 %all-to-all-start.1 = ((bf16[128,16,128]{2,1,0:T(8,128)(2,1)}), bf16[128,16,128]{2,1,0:T(8,128)(2,1)S(1)}, u32[]{:S(2)}, u32[]{:S(2)}) async-start(bf16[128,16,128]{2,1,0:T(8,128)(2,1)} %bitcast.20), calls=%async_computation.1 | async-start | bytes 1048576 | tf_op jit(solution)/shard_map/all_to_all | solution.py:434
  24.3 19.7 %collective-permute-start = (bf16[1,2,704,128]{3,2,1,0:T(8,128)(2,1)S(1)}, bf16[1,2,704,128]{3,2,1,0:T(8,128)(2,1)S(1)}, u32[]{:S(2)}, u32[]{:S(2)}) collective-permute-start(bf16[1,2,704,128]{3,2,1,0:T(8,128)(2,1)S(1)} %shard_map.73), channel_id=1, source_target_pairs={{0,1},{2,3},{4,5},{6,7},{8,9},{10,11},{12,13},{14,15},{16,17},{18,... | collective-permute-start | bytes 1081352 | tf_op jit(solution)/shard_map/ppermute | solution.py:445
  31.1 12.9 %copy-start.3 = (bf16[256,256]{1,0:T(8,128)(2,1)S(1)}, bf16[256,256]{1,0:T(8,128)(2,1)}, u32[]{:S(2)}) copy-start(bf16[256,256]{1,0:T(8,128)(2,1)} %constant.17.clone.inner_hbm.inner_ref) | copy-start | bytes 393220
  47.9 15.3 %copy-start.5 = (s32[512]{0:T(512)S(1)}, s32[512]{0:T(512)}, u32[]{:S(2)}) copy-start(s32[512]{0:T(512)} %param.10) | copy-start | bytes 6148
  47.9 15.6 %copy-start.4 = (s32[64,512]{1,0:T(8,128)S(1)}, s32[64,512]{1,0:T(8,128)}, u32[]{:S(2)}) copy-start(s32[64,512]{1,0:T(8,128)} %param.9) | copy-start | bytes 393220
  47.9 56.1 %all-to-all-start = ((bf16[128,48,128]{2,1,0:T(8,128)(2,1)}), bf16[128,48,128]{2,1,0:T(8,128)(2,1)S(1)}, u32[]{:S(2)}, u32[]{:S(2)}) async-start(bf16[128,48,128]{2,1,0:T(8,128)(2,1)} %bitcast.18), calls=%async_computation | async-start | bytes 3145728 | tf_op jit(solution)/shard_map/all_to_all | solution.py:434

commit v3 on v2

v3 whole, which is shorter than its diff:
```python
import functools

import jax
import jax.numpy as jnp
import ml_dtypes
import numpy as np
from jax import lax
from jax.experimental import pallas as pl
from jax.experimental.pallas import tpu as pltpu
from jax.sharding import PartitionSpec as P

RADIX_A = 32
RADIX_B = 128
TAPS = 12
LENGTH = RADIX_A * RADIX_B
ROWS = 2 * RADIX_A
PAIR = 2
QUAD = 2 * PAIR
EARLY = 6
BF16 = jnp.bfloat16
F32 = jnp.float32
VMEM_LIMIT = 16 << 20


def params():
    return pltpu.CompilerParams(vmem_limit_bytes=VMEM_LIMIT)


def in_hbm(array):
    return pltpu.with_memory_space_constraint(array, pltpu.HBM)


IN_VMEM = pl.BlockSpec(memory_space=pltpu.VMEM)
IN_HBM = pl.BlockSpec(memory_space=pltpu.HBM)
LIGHT = pl.CostEstimate(flops=1024, bytes_accessed=1024, transcendentals=0)
HEAVY = pl.CostEstimate(flops=1 << 37, bytes_accessed=1024, transcendentals=0)


def dft_table(radix):
    indices = np.arange(radix)
    angles = (indices[:, None] * indices[None, :] % radix) * (2.0 * np.pi / radix)
    cosine = np.cos(angles).astype(ml_dtypes.bfloat16)
    sine = np.sin(angles).astype(ml_dtypes.bfloat16)
    return np.stack(
        [np.stack([cosine, -sine], axis=1), np.stack([sine, cosine], axis=1)], axis=0
    )


def outer_table():
    table = dft_table(RADIX_A).transpose(2, 3, 1, 0)
    table = table.reshape(2, RADIX_A // 4, 4, RADIX_A, 2)
    grid = np.zeros((2, RADIX_A // 4, PAIR, 4, 2, 2, PAIR, RADIX_A, 2), ml_dtypes.bfloat16)
    for spectrum in range(PAIR):
        for pol in range(2):
            grid[:, :, spectrum, :, pol, pol, spectrum] = table
    return grid.reshape(2 * RADIX_A * QUAD, QUAD * ROWS)


def inner_table():
    return dft_table(RADIX_B).reshape(2 * RADIX_B, 2 * RADIX_B).T.copy()


def twiddles():
    c1 = np.zeros((RADIX_A // 4, PAIR, 4, 2), np.int64)
    c1 += np.arange(RADIX_A).reshape(RADIX_A // 4, 1, 4, 1)
    angles = (c1.reshape(-1, 1) * np.arange(RADIX_B) % LENGTH) * (2.0 * np.pi / LENGTH)
    scale = 1.0 / np.sqrt(np.float64(LENGTH))
    return np.stack([np.cos(angles) * scale, np.sin(angles) * scale]).astype(np.float32)


def spread_taps(taps_ref, taps2):
    for a in range(RADIX_A):
        for k in range(TAPS):
            row = taps_ref[k : k + 1, a * RADIX_B : (a + 1) * RADIX_B]
            taps2[k, 2 * a : 2 * a + 2, :] = jnp.broadcast_to(row, (2, RADIX_B))


def fir(first, count, base, stations, x_ref, near_ref, far_ref, taps2, filt, place):
    pieces = ROWS // 16

    def step(at, carry):
        station = at // (2 * pieces)
        pol = at // pieces % 2
        row = pl.multiple_of(at % pieces * 16, 16)
        frames = []
        for f in range(first - TAPS + 1, first + count):
            if f < -1:
                where = pl.multiple_of((f + TAPS - 1) * ROWS + row, 16)
                piece = far_ref[station, pol, pl.ds(where, 16), :]
            elif f < 0:
                piece = near_ref[base + station, pol, pl.ds(row, 16), :]
            else:
                where = pl.multiple_of(f * ROWS + row, 16)
                piece = x_ref[base + station, pol, pl.ds(where, 16), :]
            frames.append(piece.astype(F32))
        taps = [taps2[k, pl.ds(row, 16), :] for k in range(TAPS)]
        halves = []
        for half in range(2):
            rows = slice(8 * half, 8 * half + 8)
            outs = []
            for t in range(count):
                total = taps[0][rows] * frames[t][rows]
                for k in range(1, TAPS):
                    total = total + taps[k][rows] * frames[t + k][rows]
                outs.append(total)
            halves.append(outs)
        for t in range(count):
            both = jnp.concatenate([halves[0][t], halves[1][t]], axis=0).astype(BF16)
            where = pl.multiple_of(place(station, pol, t) * ROWS + row, 16)
            filt[pl.ds(where, 16), :] = both
        return carry

    lax.fori_loop(0, stations * 2 * pieces, step, 0)


def outer_stage(quads, stations, frame, outer_ref, tw_ref, mid):
    half = RADIX_A * QUAD
    cosine = tw_ref[0]
    sine = tw_ref[1]
    table = outer_ref[...]
    for first in range(0, stations * quads, 2):
        held = range(first, min(first + 2, stations * quads))
        data = []
        for n in held:
            s, q = n // quads, n % quads
            data.append([frame(s, pol, PAIR * q + t) for pol in range(2) for t in range(PAIR)])
        data = jnp.concatenate([jnp.concatenate(frames, axis=0) for frames in data], axis=1)
        got = jnp.dot(table, data, preferred_element_type=F32)
        for side, n in enumerate(held):
            s, q = n // quads, n % quads
            real = got[:half, side * 128 : side * 128 + 128]
            imag = got[half:, side * 128 : side * 128 + 128]
            real_out = (real * cosine + imag * sine).astype(BF16)
            imag_out = (imag * cosine - real * sine).astype(BF16)
            for g in range(half // 16):
                to = (s * half // 16 * quads + g * quads + q) * 16
                mid[to : to + 16, :RADIX_B] = real_out[16 * g : 16 * g + 16]
                mid[to : to + 16, RADIX_B:] = imag_out[16 * g : 16 * g + 16]


def inner_stage(quads, station, data_ref, start, inner_ref, turn):
    block = 8 * quads
    for first in range(0, quads, 2):
        wide = min(2, quads - first)
        at = start + first * 128
        got = lax.dot_general(
            inner_ref[...],
            data_ref[at : at + wide * 128, :],
            (((1,), (1,)), ((), ())),
            preferred_element_type=F32,
        )
        for side in range(wide):
            group = first + side
            for part in range(2):
                for c in range(0, RADIX_B, 8):
                    to = c * block + group * 8 + part + 2 * station
                    turn[pl.ds(to, 8, stride=block), :] = got[
                        part * RADIX_B + c : part * RADIX_B + c + 8,
                        side * 128 : side * 128 + 128,
                    ]


def send_out(turn, packed, out_ref, sems, before=None, station=0):
    rows = turn.shape[0]
    parts = sems.shape[0]
    size = rows // parts
    own = lax.broadcasted_iota(jnp.int32, (size, 128), 0) % 8 >= 2 * station
    copies = []
    for p in range(parts):
        part = pl.ds(p * size, size)
        values = turn[part, :]
        if before is not None:
            values = jnp.where(own, values, before[part, :])
        packed[part, :] = values.astype(BF16)
        copy = pltpu.make_async_copy(packed.at[part], out_ref.at[part], sems.at[p])
        copy.start()
        copies.append(copy)
    for copy in copies:
        copy.wait()


def fetch(pairs, sems):
    copies = [pltpu.make_async_copy(a, b, sems.at[i]) for i, (a, b) in enumerate(pairs)]
    for copy in copies:
        copy.start()
    return copies


def rows_of(filt, block):
    return filt[block * ROWS : (block + 1) * ROWS, :]


def first_body(first, count, stations, x_ref, taps2, filt):
    fir(first, count, 0, stations, x_ref, None, None, taps2, filt, lambda s, pol, t: (s * 2 + pol) * count + t)


def early_body(
    first, count, quads, stations, x_ref, near_ref, taps2, before, outer_hbm, tw_hbm, inner_hbm, out_ref,
    outer_ref, tw_ref, inner_ref, filt, mid, turn, packed, sems, in_sems,
):
    copies = fetch([(outer_hbm, outer_ref), (tw_hbm, tw_ref), (inner_hbm, inner_ref)], in_sems)
    fir(first, 1, 0, stations, x_ref, near_ref, None, taps2, filt, lambda s, pol, t: s * 2 + pol)
    for copy in copies:
        copy.wait()

    def frame(s, pol, t):
        if t == 0:
            return rows_of(filt, s * 2 + pol)
        return rows_of(before, (s * 2 + pol) * (count - 1) + t - 1)

    outer_stage(quads, stations, frame, outer_ref, tw_ref, mid)
    for s in range(stations):
        inner_stage(quads, s, mid, s * 128 * quads, inner_ref, turn)
    send_out(turn, packed, out_ref, sems)


def late_body(
    last, count, quads, base, stations, x_ref, near_ref, far_ref, taps2, outer_hbm, tw_hbm, inner_hbm, *refs
):
    if last:
        before, out_ref, outer_ref, tw_ref, inner_ref, filt, mid, in_sems, turn, packed, sems = refs
    else:
        turn, outer_ref, tw_ref, inner_ref, filt, mid, in_sems = refs

    def place(s, pol, t):
        return (s * 2 + pol) * count + t

    copies = fetch([(outer_hbm, outer_ref), (tw_hbm, tw_ref), (inner_hbm, inner_ref)], in_sems)
    fir(0, count, base, stations, x_ref, near_ref, far_ref, taps2, filt, place)
    for copy in copies:
        copy.wait()
    outer_stage(quads, stations, lambda *at: rows_of(filt, place(*at)), outer_ref, tw_ref, mid)
    for s in range(stations):
        inner_stage(quads, base + s, mid, s * 128 * quads, inner_ref, turn)
    if last:
        send_out(turn, packed, out_ref, sems, before, base)


def filter_first(x, taps2, first, count):
    stations = x.shape[0]
    return pl.pallas_call(
        functools.partial(first_body, first, count, stations),
        out_shape=jax.ShapeDtypeStruct((stations * 2 * count * ROWS, RADIX_B), BF16),
        in_specs=[IN_VMEM, IN_VMEM],
        out_specs=IN_VMEM,
        compiler_params=params(),
        cost_estimate=LIGHT,
    )(x, taps2)


def channelise_early(x, near, taps2, before, tables, first, count):
    stations = x.shape[0]
    quads = 2 * count // QUAD
    rows = RADIX_B * 8 * quads
    return pl.pallas_call(
        functools.partial(early_body, first, count, quads, stations),
        out_shape=pltpu.HBM((rows, 128), BF16),
        in_specs=[IN_VMEM] * 4 + [IN_HBM] * 3,
        out_specs=IN_HBM,
        scratch_shapes=[pltpu.VMEM(table.shape, table.dtype) for table in tables]
        + [
            pltpu.VMEM((stations * 2 * ROWS, RADIX_B), BF16),
            pltpu.VMEM((stations * 128 * quads, 2 * RADIX_B), BF16),
            pltpu.VMEM((rows, 128), F32),
            pltpu.VMEM((rows, 128), BF16),
            pltpu.SemaphoreType.DMA((4,)),
            pltpu.SemaphoreType.DMA((3,)),
        ],
        compiler_params=params(),
        cost_estimate=HEAVY,
    )(x, near, taps2, before, *map(in_hbm, tables))


def channelise_late(x, near, far, taps2, tables, base, count, before=None):
    stations = far.shape[0]
    quads = 2 * count // QUAD
    rows = RADIX_B * 8 * quads
    last = before is not None
    scratch = [pltpu.VMEM(table.shape, table.dtype) for table in tables] + [
        pltpu.VMEM((stations * 2 * count * ROWS, RADIX_B), BF16),
        pltpu.VMEM((stations * 128 * quads, 2 * RADIX_B), BF16),
        pltpu.SemaphoreType.DMA((3,)),
    ]
    if last:
        scratch += [
            pltpu.VMEM((rows, 128), F32),
            pltpu.VMEM((rows, 128), BF16),
            pltpu.SemaphoreType.DMA((8,)),
        ]
    return pl.pallas_call(
        functools.partial(late_body, last, count, quads, base, stations),
        out_shape=pltpu.HBM((rows, 128), BF16) if last else jax.ShapeDtypeStruct((rows, 128), F32),
        in_specs=[IN_VMEM] * 4 + [IN_HBM] * 3 + [IN_VMEM] * last,
        out_specs=IN_HBM if last else IN_VMEM,
        scratch_shapes=scratch,
        compiler_params=params(),
        cost_estimate=HEAVY,
    )(x, near, far, taps2, *map(in_hbm, tables), *([before] if last else []))


def history_body(starts, x_ref, *refs):
    count = len(starts)
    taps_ref = taps2 = None
    if len(refs) > 2 * count + 2:
        taps_hbm, refs = refs[0], refs[1:]
        taps2 = refs[count]
        refs = refs[:count] + refs[count + 1 :]
        taps_ref, taps_sem, refs = refs[-2], refs[-1], refs[:-2]
        taps_copy = pltpu.make_async_copy(taps_hbm, taps_ref, taps_sem)
        taps_copy.start()
    outs, helds, sems, out_sems = refs[:count], refs[count : 2 * count], refs[-2], refs[-1]
    pieces = []
    for (station, start), out, held in zip(starts, outs, helds):
        for s in range(out.shape[0]):
            at = len(pieces)
            source = x_ref.at[station + s, :, pl.ds(start, out.shape[2])]
            into = pltpu.make_async_copy(source, held.at[s], sems.at[at])
            onward = pltpu.make_async_copy(held.at[s], out.at[s], out_sems.at[at])
            into.start()
            pieces.append((into, onward))
    for into, onward in pieces:
        into.wait()
        onward.start()
    if taps_ref is not None:
        taps_copy.wait()
        spread_taps(taps_ref, taps2)
    for _, onward in pieces:
        onward.wait()


def history(x, parts, taps=None):
    shapes = [(n, 2, frames * ROWS, RADIX_B) for _, n, _, frames in parts]
    starts = [(station, frame * ROWS) for station, _, frame, _ in parts]
    pieces = sum(n for _, n, _, _ in parts)
    operands, in_specs, fetch = [in_hbm(x)], [IN_HBM], []
    out_shape = [pltpu.HBM(shape, BF16) for shape in shapes]
    out_specs = [IN_HBM] * len(parts)
    if taps is not None:
        operands.append(in_hbm(taps))
        in_specs.append(IN_HBM)
        fetch = [pltpu.VMEM(taps.shape, F32), pltpu.SemaphoreType.DMA]
        out_shape.append(jax.ShapeDtypeStruct((TAPS, ROWS, RADIX_B), F32))
        out_specs.append(IN_VMEM)
    return pl.pallas_call(
        functools.partial(history_body, starts),
        out_shape=out_shape,
        in_specs=in_specs,
        out_specs=out_specs,
        scratch_shapes=[pltpu.VMEM(shape, BF16) for shape in shapes]
        + [pltpu.SemaphoreType.DMA((pieces,))] * 2
        + fetch,
        compiler_params=params(),
        cost_estimate=LIGHT,
    )(*operands)


def weights_body(upper_ref, codes_ref, scale_ref, hbm_ref, out_ref, sem):
    upper = upper_ref[0]
    unit = 2.0 * np.pi / LENGTH

    def step(at, carry):
        row = pl.multiple_of(at // 8 * 16, 16)
        col = pl.multiple_of(at % 8 * 128, 128)
        codes = codes_ref[pl.ds(row, 16), pl.ds(col, 128)]
        scale = scale_ref[:, pl.ds(col, 128)]
        start = ((codes * (upper * RADIX_A)) & (LENGTH - 1)).astype(F32) * unit
        by = codes.astype(F32) * unit
        odd = (lax.broadcasted_iota(jnp.int32, (16, 128), 1) & 1) == 1
        cosine = jnp.cos(start) * scale
        sine = jnp.sin(start) * scale
        here = jnp.where(odd, sine, cosine)
        across = jnp.where(odd, cosine, -sine)
        by_cos = jnp.cos(by)
        by_sin = jnp.sin(by)
        for c1 in range(RADIX_A):
            out_ref[c1, pl.ds(row, 16), pl.ds(col, 128)] = here.astype(BF16)
            if c1 + 1 < RADIX_A:
                here, across = here * by_cos + across * by_sin, across * by_cos - here * by_sin
        return carry

    lax.fori_loop(0, 32, step, 0)
    copy = pltpu.make_async_copy(out_ref, hbm_ref, sem)
    copy.start()
    copy.wait()


def beam_weights(upper, codes, flags):
    beam_count, stations = codes.shape
    codes = jnp.repeat(codes, 2, axis=1)
    scale = flags.astype(F32) / jnp.sqrt(jnp.float32(stations))
    scale = jnp.repeat(scale, 2)[None, :]
    shape = (RADIX_A, beam_count, 2 * stations)
    return pl.pallas_call(
        weights_body,
        out_shape=pltpu.HBM(shape, BF16),
        in_specs=[pl.BlockSpec(memory_space=pltpu.SMEM), IN_VMEM, IN_VMEM],
        out_specs=IN_HBM,
        scratch_shapes=[pltpu.VMEM(shape, BF16), pltpu.SemaphoreType.DMA],
        compiler_params=params(),
        cost_estimate=LIGHT,
    )(upper, codes, scale)


def beams_body(quads, last, x_ref, w_hbm, *refs):
    if last:
        early_ref, out_ref, total, w_ref, sems = refs
    else:
        out_ref, w_ref, sems = refs
        total = out_ref
    copies = []
    for g in range(RADIX_A // 4):
        part = pl.ds(4 * g, 4)
        copies.append(pltpu.make_async_copy(w_hbm.at[part], w_ref.at[part], sems.at[g]))
        copies[g].start()
    waited = 0
    beam_count = w_ref.shape[1]
    spectra = total.shape[0] // (2 * RADIX_A)
    if last:
        early = early_ref.shape[0] // (2 * RADIX_A)
        for t in range(early):
            for row in range(0, 2 * RADIX_A, 8):
                total[pl.ds((row + 1) * spectra - early + t, 8, stride=spectra), :] = early_ref[
                    pl.ds(row * early + t, 8, stride=early), :
                ]
    lane = lax.broadcasted_iota(jnp.int32, (1, 128), 1)
    even = (lax.broadcasted_iota(jnp.int32, (1, 8, 128), 1) & 1) == 0
    for group in range(quads):
        base = group * 128
        low = base // (16 * quads)
        high = (base + 127) // (16 * quads)
        values = x_ref[:, group]
        wide = values.astype(F32)
        swapped = jnp.where(even, pltpu.roll(wide, 7, 1), -pltpu.roll(wide, 1, 1)).astype(BF16)
        data = jnp.concatenate([values.reshape(1024, 128), swapped.reshape(1024, 128)], axis=1)
        c1 = (base + lane) // (16 * quads) * 4 + lane % 8 // 2
        real = imag = None
        for g in range(low, high + 1):
            while waited <= g:
                copies[waited].wait()
                waited += 1
            weights = w_ref[4 * g : 4 * g + 4].reshape(4 * beam_count, 1024)
            got = jnp.dot(weights, data, preferred_element_type=F32)
            for c in range(4):
                piece = got[beam_count * c : beam_count * (c + 1)]
                if real is None:
                    real, imag = piece[:, :128], piece[:, 128:]
                else:
                    mine = c1 == 4 * g + c
                    real = jnp.where(mine, piece[:, :128], real)
                    imag = jnp.where(mine, piece[:, 128:], imag)
        turned = jnp.concatenate([real, imag], axis=0).T
        for m in range(0, 128, 8):
            at = base + m
            block = at // (16 * quads)
            t = at % (16 * quads) // 16 * PAIR + at % 16 // 8
            total[pl.ds(block * 8 * spectra + t, 8, stride=spectra), :] = turned[m : m + 8]
    if last:
        out_ref[...] = total[...].astype(BF16)


def beams(received, weights, quads, early):
    count = quads * QUAD // 2
    received = received.reshape(RADIX_B, quads, 8, 128)
    operands = [received, in_hbm(weights)]
    in_specs = [IN_VMEM, IN_HBM]
    scratch = [pltpu.VMEM(weights.shape, BF16), pltpu.SemaphoreType.DMA((RADIX_A // 4,))]
    last = early is not None
    if last:
        operands.append(early)
        in_specs.append(IN_VMEM)
        shape = (2 * RADIX_A * count + early.shape[0], 128)
        out_shape = jax.ShapeDtypeStruct(shape, BF16)
        scratch = [pltpu.VMEM(shape, F32)] + scratch
    else:
        out_shape = jax.ShapeDtypeStruct((2 * RADIX_A * count, 128), F32)
    return pl.pallas_call(
        functools.partial(beams_body, quads, last),
        out_shape=out_shape,
        in_specs=in_specs,
        out_specs=IN_VMEM,
        scratch_shapes=scratch,
        compiler_params=params(),
        cost_estimate=LIGHT,
    )(*operands)


def turn(spectra):
    spectra = spectra.reshape(RADIX_B, -1, 128)
    return lax.all_to_all(spectra, "stn", split_axis=0, concat_axis=0, tiled=True)


def shards(samples, taps, codes, flags):
    stations = samples.shape[0]
    frames = samples.shape[3] // LENGTH
    size = lax.axis_size("tm")
    x = samples.reshape(stations, 2, 2, frames * RADIX_A, RADIX_B)
    x = x.transpose(0, 1, 3, 2, 4).reshape(stations, 2, frames * ROWS, RADIX_B)
    pairs = [(i, i + 1) for i in range(size - 1)]
    lead = stations - 1
    rest = frames - TAPS + 1, TAPS - 2
    parts = [(0, stations, frames - 1, 1), (0, lead, *rest), (lead, 1, *rest)]
    near, far, far_last, taps2 = history(x, parts, taps)
    near = lax.ppermute(near, "tm", pairs)
    far = lax.ppermute(far, "tm", pairs)

    tables = (jnp.asarray(outer_table()), jnp.asarray(twiddles()), jnp.asarray(inner_table()))
    late = frames - EARLY
    filtered = filter_first(x, taps2, late + 1, EARLY - 1)
    early_sent = channelise_early(x, near, taps2, filtered, tables, late, EARLY)
    early_sent, far_last = lax.optimization_barrier((early_sent, far_last))
    early_got = turn(early_sent)
    far_last = lax.ppermute(far_last, "tm", pairs)
    upper = lax.axis_index("stn").astype(jnp.int32).reshape(1)
    weights = beam_weights(upper, codes, flags)
    ahead = channelise_late(x, near, far, taps2, tables, 0, late)
    main_sent = channelise_late(x, near, far_last, taps2, tables, lead, late, ahead)
    main_got = turn(main_sent)
    early = beams(early_got, weights, EARLY // PAIR, None)
    result = beams(main_got, weights, late // PAIR, early)
    return result.reshape(RADIX_A, 2, frames, 128)


def solution(mesh):
    in_specs = (P("stn", None, None, "tm"), P(), P(), P())
    out_specs = P("stn", None, "tm", None)
    return jax.shard_map(shards, mesh=mesh, in_specs=in_specs, out_specs=out_specs, check_vma=False)
```

time: 111 us -> 107 us (0.964)
  Pallas kernels: 35.4 us -> 33.5 us
  waiting for transfers between devices: 41.4 us -> 39.7 us
    all_to_all x2, waiting for transfers between devices: 27.9 us -> 24.5 us  [turn(): lax.all_to_all(spectra, 'stn', split_axis=0, concat_axis=0, tiled=True)]
    all_to_all x2, starting transfers between devices: 29.6 us -> 27.5 us  [turn(): lax.all_to_all(spectra, 'stn', split_axis=0, concat_axis=0, tiled=True)]
    pallas_call x1, Pallas kernels: 5.19 us -> 3.16 us  [channelise_early(): pl.pallas_call(functools.partial(early_body, first, count, quads, station...]
    ppermute x2 -> x3, waiting for transfers between devices: 13.4 us -> 15.2 us  [the longest x1 12 us: shards(): far_last = lax.ppermute(far_last, 'tm', pairs)]
    ppermute x2 -> x3, starting transfers between devices: 2.58 us -> 3.88 us  [the longest x1 1.29 us: shards(): near = lax.ppermute(near, 'tm', pairs)]
  transfers between devices with their start and end apart: 4 -> 5, of which waited for: 3 -> 5; matrix products, arithmetic and copies ran while one was open for 1% -> 1% of each run, Pallas kernels for 25% -> 24%
where the time goes in v3:
time: 107 us
  waiting for transfers between devices  39.7 us (37%)
  Pallas kernels  33.5 us (31%)
  starting transfers between devices  31.4 us (29%)
  local copies, waits for them, and re-layouts  1.71 us (2%)
    all_to_all x2, starting transfers between devices, turn(): lax.all_to_all(spectra, 'stn', split_axis=0, concat_axis=0, tiled=True)  27.5 us
    all_to_all x2, waiting for transfers between devices, turn(): lax.all_to_all(spectra, 'stn', split_axis=0, concat_axis=0, tiled=True)  24.5 us
    ppermute x1, waiting for transfers between devices, shards(): far_last = lax.ppermute(far_last, 'tm', pairs)  12 us
    pallas_call x2, Pallas kernels, beams(): pl.pallas_call(functools.partial(beams_body, quads, last), out_shape=out_...  11.6 us
    pallas_call x1, Pallas kernels, beam_weights(): pl.pallas_call(weights_body, out_shape=pltpu.HBM(shape, BF16), in_specs=[...  7.22 us
    pallas_call x2, Pallas kernels, channelise_late(): pl.pallas_call(functools.partial(late_body, last, count, quads, base, sta...  6.79 us
    pallas_call x1, Pallas kernels, channelise_early(): pl.pallas_call(functools.partial(early_body, first, count, quads, station...  3.16 us
    ppermute x1, waiting for transfers between devices, shards(): near = lax.ppermute(near, 'tm', pairs)  3.08 us
  transfers between devices with their start and end apart: 5, of which 5 were waited for; matrix products, arithmetic and copies ran while one was open for 1% of the time, Pallas kernels for 24%

profile of v3, /device:TPU:7, one launch (start us, length us, event | category | flops | bytes accessed | tf_op | source)
XLA Modules:
  0.0 106.7 jit_solution(8610931112381353711)
XLA Ops:
  0.0 0.0 copy-start
  0.0 2.5 %shard_map.73 = (bf16[4,2,64,128]{3,2,1,0:T(8,128)(2,1)}, bf16[3,2,640,128]{3,2,1,0:T(8,128)(2,1)}, bf16[1,2,640,128]{3,2,1,0:T(8,128)(2,1)}, f32[12,64,128]{2,1,0:T(8,128)S(1)}) custom-call(bf16[4,2,1024,128]{3,2,1,0:T(8,128)(2,1)} %bitcast.12, f32[12,4096]{1,0:T(8,128)} %refs_0_.1), custom_call_target="tpu_custom_call" | custom-call | flops 1024 | bytes 1024 | tf_op jit(solution)/shard_map/pallas_call | solution.py:344
  2.5 1.3 %collective-permute-start = (bf16[4,2,64,128]{3,2,1,0:T(8,128)(2,1)}, bf16[4,2,64,128]{3,2,1,0:T(8,128)(2,1)S(1)}, u32[]{:S(2)}, u32[]{:S(2)}) collective-permute-start(bf16[4,2,64,128]{3,2,1,0:T(8,128)(2,1)} %get-tuple-element.11), channel_id=1, source_target_pairs={{0,1},{2,3},{4,5},{6,7},{8,9},{10,11},{12,13},{14,15},{16,17},{18,... | collective-permute-start | bytes 393224 | tf_op jit(solution)/shard_map/ppermute | solution.py:503
  3.8 1.3 %collective-permute-start.2 = (bf16[3,2,640,128]{3,2,1,0:T(8,128)(2,1)}, bf16[3,2,640,128]{3,2,1,0:T(8,128)(2,1)S(1)}, u32[]{:S(2)}, u32[]{:S(2)}) collective-permute-start(bf16[3,2,640,128]{3,2,1,0:T(8,128)(2,1)} %get-tuple-element.15), channel_id=1, source_target_pairs={{0,1},{2,3},{4,5},{6,7},{8,9},{10,11},{12,13},{14,15},{16,17},{18,... | collective-permute-start | bytes 2949128 | tf_op jit(solution)/shard_map/ppermute | solution.py:504
  5.1 0.0 copy-done
  5.1 2.3 %shard_map.74.before = bf16[2560,128]{1,0:T(8,128)(2,1)S(1)} custom-call(bf16[4,2,1024,128]{3,2,1,0:T(8,128)(2,1)S(1)} %bitcast.13, f32[12,64,128]{2,1,0:T(8,128)S(1)} %get-tuple-element.12.taps2), custom_call_target="tpu_custom_call" | custom-call | flops 1024 | bytes 1024 | tf_op jit(solution)/shard_map/pallas_call | solution.py:241
  7.4 3.1 %collective-permute-done.near_ref = bf16[4,2,64,128]{3,2,1,0:T(8,128)(2,1)S(1)} collective-permute-done((bf16[4,2,64,128]{3,2,1,0:T(8,128)(2,1)}, bf16[4,2,64,128]{3,2,1,0:T(8,128)(2,1)S(1)}, u32[]{:S(2)}, u32[]{:S(2)}) %collective-permute-start) | collective-permute-done | bytes 131104 | tf_op jit(solution)/shard_map/ppermute | solution.py:503
  10.4 0.0 copy-start.1
  10.4 3.2 %shard_map.75 = bf16[3072,128]{1,0:T(8,128)(2,1)} custom-call(bf16[4,2,1024,128]{3,2,1,0:T(8,128)(2,1)S(1)} %bitcast.14, bf16[4,2,64,128]{3,2,1,0:T(8,128)(2,1)S(1)} %collective-permute-done.near_ref, f32[12,64,128]{2,1,0:T(8,128)S(1)} %get-tuple-element.12.taps2, bf16[2560,128]{1,0:T(8,128)(2,1)S(1)} %shard_map.74.before, ...), custom_call_target="tpu_custom_call" | custom-call | flops 137438953472 | bytes 1024 | tf_op jit(solution)/shard_map/pallas_call | solution.py:255
  13.6 0.0 copy-done.1
  13.6 16.6 %all-to-all-start.1 = ((bf16[128,24,128]{2,1,0:T(8,128)(2,1)}), bf16[128,24,128]{2,1,0:T(8,128)(2,1)}, u32[]{:S(2)}, u32[]{:S(2)}) async-start(bf16[128,24,128]{2,1,0:T(8,128)(2,1)} %bitcast.20), calls=%async_computation.1 | async-start | bytes 1572864 | tf_op jit(solution)/shard_map/all_to_all | solution.py:489
  30.3 1.3 %collective-permute-start.1 = (bf16[1,2,640,128]{3,2,1,0:T(8,128)(2,1)}, bf16[1,2,640,128]{3,2,1,0:T(8,128)(2,1)S(1)}, u32[]{:S(2)}, u32[]{:S(2)}) collective-permute-start(bf16[1,2,640,128]{3,2,1,0:T(8,128)(2,1)} %get-tuple-element.14), channel_id=1, source_target_pairs={{0,1},{2,3},{4,5},{6,7},{8,9},{10,11},{12,13},{14,15},{16,17},{18,... | collective-permute-start | bytes 983048 | tf_op jit(solution)/shard_map/ppermute | solution.py:512
  31.6 0.1 collective-permute-done.2.far_ref
  31.7 0.9 copy-done.2
  32.6 3.8 %shard_map.76.refs_0_ = f32[5120,128]{1,0:T(8,128)S(1)} custom-call(bf16[4,2,1024,128]{3,2,1,0:T(8,128)(2,1)S(1)} %bitcast.15, bf16[4,2,64,128]{3,2,1,0:T(8,128)(2,1)S(1)} %copy-done.2, bf16[3,2,640,128]{3,2,1,0:T(8,128)(2,1)S(1)} %collective-permute-done.2.far_ref, f32[12,64,128]{2,1,0:T(8,128)S(1)} %get-tuple-element.12.taps2, ...), custom_call_target="tpu_custom_call" | custom-call | flops 137438953472 | bytes 1024 | tf_op jit(solution)/shard_map/pallas_call | solution.py:290
  36.4 12.0 %collective-permute-done.1.far_ref = bf16[1,2,640,128]{3,2,1,0:T(8,128)(2,1)S(1)} collective-permute-done((bf16[1,2,640,128]{3,2,1,0:T(8,128)(2,1)}, bf16[1,2,640,128]{3,2,1,0:T(8,128)(2,1)S(1)}, u32[]{:S(2)}, u32[]{:S(2)}) %collective-permute-start.1) | collective-permute-done | bytes 327712 | tf_op jit(solution)/shard_map/ppermute | solution.py:512
  48.4 3.0 %shard_map.77 = bf16[5120,128]{1,0:T(8,128)(2,1)} custom-call(bf16[4,2,1024,128]{3,2,1,0:T(8,128)(2,1)S(1)} %bitcast.16, bf16[4,2,64,128]{3,2,1,0:T(8,128)(2,1)S(1)} %copy-done.2, bf16[1,2,640,128]{3,2,1,0:T(8,128)(2,1)S(1)} %collective-permute-done.1.far_ref, f32[12,64,128]{2,1,0:T(8,128)S(1)} %get-tuple-element.12.taps2, ...), custom_call_target="tpu_custom_call" | custom-call | flops 137438953472 | bytes 1024 | tf_op jit(solution)/shard_map/pallas_call | solution.py:290
  51.5 0.0 copy-start.4
  51.5 0.0 copy-start.3
  51.5 2.9 %all-to-all-done.1 = bf16[128,24,128]{2,1,0:T(8,128)(2,1)} async-done(((bf16[128,24,128]{2,1,0:T(8,128)(2,1)}), bf16[128,24,128]{2,1,0:T(8,128)(2,1)}, u32[]{:S(2)}, u32[]{:S(2)}) %all-to-all-start.1) | async-done | bytes 786464 | tf_op jit(solution)/shard_map/all_to_all | solution.py:489
  54.4 10.9 %all-to-all-start = ((bf16[128,40,128]{2,1,0:T(8,128)(2,1)}), bf16[128,40,128]{2,1,0:T(8,128)(2,1)S(1)}, u32[]{:S(2)}, u32[]{:S(2)}) async-start(bf16[128,40,128]{2,1,0:T(8,128)(2,1)} %bitcast.19), calls=%async_computation | async-start | bytes 2621440 | tf_op jit(solution)/shard_map/all_to_all | solution.py:489
  65.3 0.0 copy-done.4
  65.3 0.1 broadcast_in_dim.7
  65.4 0.2 broadcast_in_dim_reshape.3.scale_ref
  65.6 0.0 copy-done.3
  65.6 0.1 copy.10
  65.8 0.2 broadcast_in_dim.6
  66.0 0.2 copy.11.codes_ref
  66.1 7.2 %shard_map.78.w_hbm = bf16[32,64,1024]{2,1,0:T(8,128)(2,1)} custom-call(s32[1]{0:T(128)} %bitcast.7.upper_ref, s32[64,1024]{1,0:T(8,128)S(1)} %copy.11.codes_ref, f32[1,1024]{1,0:T(1,128)S(1)} %broadcast_in_dim_reshape.3.scale_ref), custom_call_target="tpu_custom_call" | custom-call | flops 1024 | bytes 1024 | tf_op jit(solution)/shard_map/pallas_call | solution.py:393
  73.4 5.9 %shard_map.79.refs_0_ = f32[384,128]{1,0:T(8,128)S(1)} custom-call(bf16[128,3,8,128]{3,2,1,0:T(8,128)(2,1)} %bitcast.10.x_ref, bf16[32,64,1024]{2,1,0:T(8,128)(2,1)} %shard_map.78.w_hbm), custom_call_target="tpu_custom_call" | custom-call | flops 1024 | bytes 1024 | tf_op jit(solution)/shard_map/pallas_call | solution.py:476
  79.3 21.6 %all-to-all-done = bf16[128,40,128]{2,1,0:T(8,128)(2,1)S(1)} async-done(((bf16[128,40,128]{2,1,0:T(8,128)(2,1)}), bf16[128,40,128]{2,1,0:T(8,128)(2,1)S(1)}, u32[]{:S(2)}, u32[]{:S(2)}) %all-to-all-start) | async-done | bytes 1310752 | tf_op jit(solution)/shard_map/all_to_all | solution.py:489
  100.9 5.7 %shard_map.80 = bf16[1024,128]{1,0:T(8,128)(2,1)} custom-call(bf16[128,5,8,128]{3,2,1,0:T(8,128)(2,1)S(1)} %bitcast.17, bf16[32,64,1024]{2,1,0:T(8,128)(2,1)} %shard_map.78.w_hbm, f32[384,128]{1,0:T(8,128)S(1)} %shard_map.79.refs_0_), custom_call_target="tpu_custom_call" | custom-call | flops 1024 | bytes 1024 | tf_op jit(solution)/shard_map/pallas_call | solution.py:476
  (2 shorter events, 0.0 us)
Async XLA Ops:
  0.0 5.1 %copy-start = (bf16[4,2,2,65536]{3,2,1,0:T(2,128)(2,1)S(1)}, bf16[4,2,2,65536]{3,2,1,0:T(2,128)(2,1)}, u32[]{:S(2)}) copy-start(bf16[4,2,2,65536]{3,2,1,0:T(2,128)(2,1)} %param.7) | copy-start | bytes 6291460
  2.5 8.0 %collective-permute-start = (bf16[4,2,64,128]{3,2,1,0:T(8,128)(2,1)}, bf16[4,2,64,128]{3,2,1,0:T(8,128)(2,1)S(1)}, u32[]{:S(2)}, u32[]{:S(2)}) collective-permute-start(bf16[4,2,64,128]{3,2,1,0:T(8,128)(2,1)} %get-tuple-element.11), channel_id=1, source_target_pairs={{0,1},{2,3},{4,5},{6,7},{8,9},{10,11},{12,13},{14,15},{16,17},{18,... | collective-permute-start | bytes 393224 | tf_op jit(solution)/shard_map/ppermute | solution.py:503
  3.8 27.9 %collective-permute-start.2 = (bf16[3,2,640,128]{3,2,1,0:T(8,128)(2,1)}, bf16[3,2,640,128]{3,2,1,0:T(8,128)(2,1)S(1)}, u32[]{:S(2)}, u32[]{:S(2)}) collective-permute-start(bf16[3,2,640,128]{3,2,1,0:T(8,128)(2,1)} %get-tuple-element.15), channel_id=1, source_target_pairs={{0,1},{2,3},{4,5},{6,7},{8,9},{10,11},{12,13},{14,15},{16,17},{18,... | collective-permute-start | bytes 2949128 | tf_op jit(solution)/shard_map/ppermute | solution.py:504
  10.4 3.2 %copy-start.1 = (bf16[4,2,64,128]{3,2,1,0:T(8,128)(2,1)}, bf16[4,2,64,128]{3,2,1,0:T(8,128)(2,1)S(1)}, u32[]{:S(2)}) copy-start(bf16[4,2,64,128]{3,2,1,0:T(8,128)(2,1)S(1)} %collective-permute-done.near_ref) | copy-start | bytes 393220
  13.6 40.8 %all-to-all-start.1 = ((bf16[128,24,128]{2,1,0:T(8,128)(2,1)}), bf16[128,24,128]{2,1,0:T(8,128)(2,1)}, u32[]{:S(2)}, u32[]{:S(2)}) async-start(bf16[128,24,128]{2,1,0:T(8,128)(2,1)} %bitcast.20), calls=%async_computation.1 | async-start | bytes 1572864 | tf_op jit(solution)/shard_map/all_to_all | solution.py:489
  30.3 18.1 %collective-permute-start.1 = (bf16[1,2,640,128]{3,2,1,0:T(8,128)(2,1)}, bf16[1,2,640,128]{3,2,1,0:T(8,128)(2,1)S(1)}, u32[]{:S(2)}, u32[]{:S(2)}) collective-permute-start(bf16[1,2,640,128]{3,2,1,0:T(8,128)(2,1)} %get-tuple-element.14), channel_id=1, source_target_pairs={{0,1},{2,3},{4,5},{6,7},{8,9},{10,11},{12,13},{14,15},{16,17},{18,... | collective-permute-start | bytes 983048 | tf_op jit(solution)/shard_map/ppermute | solution.py:512
  31.7 0.9 copy-start.2
  51.5 13.8 %copy-start.4 = (s32[512]{0:T(512)S(1)}, s32[512]{0:T(512)}, u32[]{:S(2)}) copy-start(s32[512]{0:T(512)} %param.10) | copy-start | bytes 6148
  51.5 14.2 %copy-start.3 = (s32[64,512]{1,0:T(8,128)S(1)}, s32[64,512]{1,0:T(8,128)}, u32[]{:S(2)}) copy-start(s32[64,512]{1,0:T(8,128)} %param.9) | copy-start | bytes 393220
  54.4 46.5 %all-to-all-start = ((bf16[128,40,128]{2,1,0:T(8,128)(2,1)}), bf16[128,40,128]{2,1,0:T(8,128)(2,1)S(1)}, u32[]{:S(2)}, u32[]{:S(2)}) async-start(bf16[128,40,128]{2,1,0:T(8,128)(2,1)} %bitcast.19), calls=%async_computation | async-start | bytes 2621440 | tf_op jit(solution)/shard_map/all_to_all | solution.py:489

commit v4 on v3

--- a/solution.py
+++ b/solution.py
@@ -16,7 +16,9 @@
 ROWS = 2 * RADIX_A
 PAIR = 2
 QUAD = 2 * PAIR
-EARLY = 6
+KEPT = 16
+NEAR = 1
+EARLY = TAPS - 7 + NEAR
 BF16 = jnp.bfloat16
 F32 = jnp.float32
 VMEM_LIMIT = 16 << 20
@@ -33,6 +35,7 @@
 IN_VMEM = pl.BlockSpec(memory_space=pltpu.VMEM)
 IN_HBM = pl.BlockSpec(memory_space=pltpu.HBM)
 LIGHT = pl.CostEstimate(flops=1024, bytes_accessed=1024, transcendentals=0)
+SOME = pl.CostEstimate(flops=7 << 30, bytes_accessed=1024, transcendentals=0)
 HEAVY = pl.CostEstimate(flops=1 << 37, bytes_accessed=1024, transcendentals=0)
 
 
@@ -84,14 +87,15 @@
         row = pl.multiple_of(at % pieces * 16, 16)
         frames = []
         for f in range(first - TAPS + 1, first + count):
-            if f < -1:
+            if f < -NEAR:
                 where = pl.multiple_of((f + TAPS - 1) * ROWS + row, 16)
                 piece = far_ref[station, pol, pl.ds(where, 16), :]
             elif f < 0:
-                piece = near_ref[base + station, pol, pl.ds(row, 16), :]
+                where = pl.multiple_of((f + NEAR) * ROWS + row, 16)
+                piece = near_ref[base + station, pol, pl.ds(where, 16), :]
             else:
                 where = pl.multiple_of(f * ROWS + row, 16)
-                piece = x_ref[base + station, pol, pl.ds(where, 16), :]
+                piece = x_ref[station, pol, pl.ds(where, 16), :]
             frames.append(piece.astype(F32))
         taps = [taps2[k, pl.ds(row, 16), :] for k in range(TAPS)]
         halves = []
@@ -199,14 +203,14 @@
     outer_ref, tw_ref, inner_ref, filt, mid, turn, packed, sems, in_sems,
 ):
     copies = fetch([(outer_hbm, outer_ref), (tw_hbm, tw_ref), (inner_hbm, inner_ref)], in_sems)
-    fir(first, 1, 0, stations, x_ref, near_ref, None, taps2, filt, lambda s, pol, t: s * 2 + pol)
+    fir(first, NEAR, 0, stations, x_ref, near_ref, None, taps2, filt, lambda s, pol, t: (s * 2 + pol) * NEAR + t)
     for copy in copies:
         copy.wait()
 
     def frame(s, pol, t):
-        if t == 0:
-            return rows_of(filt, s * 2 + pol)
-        return rows_of(before, (s * 2 + pol) * (count - 1) + t - 1)
+        if t < NEAR:
+            return rows_of(filt, (s * 2 + pol) * NEAR + t)
+        return rows_of(before, (s * 2 + pol) * (count - NEAR) + t - NEAR)
 
     outer_stage(quads, stations, frame, outer_ref, tw_ref, mid)
     for s in range(stations):
@@ -220,7 +224,11 @@
     if last:
         before, out_ref, outer_ref, tw_ref, inner_ref, filt, mid, in_sems, turn, packed, sems = refs
     else:
-        turn, outer_ref, tw_ref, inner_ref, filt, mid, in_sems = refs
+        turn, outer_ref, tw_ref, inner_ref, filt, mid, in_sems, held, held_sem = refs
+        copy = pltpu.make_async_copy(x_ref.at[pl.ds(base, stations), :, pl.ds(0, held.shape[2])], held, held_sem)
+        copy.start()
+        copy.wait()
+        x_ref = held
 
     def place(s, pol, t):
         return (s * 2 + pol) * count + t
@@ -244,7 +252,7 @@
         in_specs=[IN_VMEM, IN_VMEM],
         out_specs=IN_VMEM,
         compiler_params=params(),
-        cost_estimate=LIGHT,
+        cost_estimate=HEAVY,
     )(x, taps2)
 
 
@@ -259,7 +267,7 @@
         out_specs=IN_HBM,
         scratch_shapes=[pltpu.VMEM(table.shape, table.dtype) for table in tables]
         + [
-            pltpu.VMEM((stations * 2 * ROWS, RADIX_B), BF16),
+            pltpu.VMEM((stations * 2 * NEAR * ROWS, RADIX_B), BF16),
             pltpu.VMEM((stations * 128 * quads, 2 * RADIX_B), BF16),
             pltpu.VMEM((rows, 128), F32),
             pltpu.VMEM((rows, 128), BF16),
@@ -267,7 +275,7 @@
             pltpu.SemaphoreType.DMA((3,)),
         ],
         compiler_params=params(),
-        cost_estimate=HEAVY,
+        cost_estimate=SOME,
     )(x, near, taps2, before, *map(in_hbm, tables))
 
 
@@ -287,15 +295,17 @@
             pltpu.VMEM((rows, 128), BF16),
             pltpu.SemaphoreType.DMA((8,)),
         ]
+    else:
+        scratch += [pltpu.VMEM((stations, 2, count * ROWS, RADIX_B), BF16), pltpu.SemaphoreType.DMA]
     return pl.pallas_call(
         functools.partial(late_body, last, count, quads, base, stations),
         out_shape=pltpu.HBM((rows, 128), BF16) if last else jax.ShapeDtypeStruct((rows, 128), F32),
-        in_specs=[IN_VMEM] * 4 + [IN_HBM] * 3 + [IN_VMEM] * last,
+        in_specs=[IN_VMEM if last else IN_HBM] + [IN_VMEM] * 3 + [IN_HBM] * 3 + [IN_VMEM] * last,
         out_specs=IN_HBM if last else IN_VMEM,
         scratch_shapes=scratch,
         compiler_params=params(),
-        cost_estimate=HEAVY,
-    )(x, near, far, taps2, *map(in_hbm, tables), *([before] if last else []))
+        cost_estimate=HEAVY if last else LIGHT,
+    )(x if last else in_hbm(x), near, far, taps2, *map(in_hbm, tables), *([before] if last else []))
 
 
 def history_body(starts, x_ref, *refs):
@@ -354,7 +364,7 @@
     )(*operands)
 
 
-def weights_body(upper_ref, codes_ref, scale_ref, hbm_ref, out_ref, sem):
+def weights_body(upper_ref, codes_ref, scale_ref, near_ref, far_hbm, far_ref, sem):
     upper = upper_ref[0]
     unit = 2.0 * np.pi / LENGTH
 
@@ -373,13 +383,14 @@
         by_cos = jnp.cos(by)
         by_sin = jnp.sin(by)
         for c1 in range(RADIX_A):
-            out_ref[c1, pl.ds(row, 16), pl.ds(col, 128)] = here.astype(BF16)
+            to_ref, at_c1 = (near_ref, c1) if c1 < KEPT else (far_ref, c1 - KEPT)
+            to_ref[at_c1, pl.ds(row, 16), pl.ds(col, 128)] = here.astype(BF16)
             if c1 + 1 < RADIX_A:
                 here, across = here * by_cos + across * by_sin, across * by_cos - here * by_sin
         return carry
 
     lax.fori_loop(0, 32, step, 0)
-    copy = pltpu.make_async_copy(out_ref, hbm_ref, sem)
+    copy = pltpu.make_async_copy(far_ref, far_hbm, sem)
     copy.start()
     copy.wait()
 
@@ -389,39 +400,32 @@
     codes = jnp.repeat(codes, 2, axis=1)
     scale = flags.astype(F32) / jnp.sqrt(jnp.float32(stations))
     scale = jnp.repeat(scale, 2)[None, :]
-    shape = (RADIX_A, beam_count, 2 * stations)
+    shape = (RADIX_A - KEPT, beam_count, 2 * stations)
     return pl.pallas_call(
         weights_body,
-        out_shape=pltpu.HBM(shape, BF16),
+        out_shape=[pltpu.VMEM((KEPT,) + shape[1:], BF16), pltpu.HBM(shape, BF16)],
         in_specs=[pl.BlockSpec(memory_space=pltpu.SMEM), IN_VMEM, IN_VMEM],
-        out_specs=IN_HBM,
+        out_specs=[IN_VMEM, IN_HBM],
         scratch_shapes=[pltpu.VMEM(shape, BF16), pltpu.SemaphoreType.DMA],
         compiler_params=params(),
         cost_estimate=LIGHT,
     )(upper, codes, scale)
 
 
-def beams_body(quads, last, x_ref, w_hbm, *refs):
-    if last:
-        early_ref, out_ref, total, w_ref, sems = refs
+def beams_body(quads, last, x_ref, near_ref, far_hbm, *refs):
+    if last:
+        early_hbm, out_ref, total, far_ref, sems, early_ref, early_sem = refs
+        early_copy = pltpu.make_async_copy(early_hbm, early_ref, early_sem)
     else:
-        out_ref, w_ref, sems = refs
-        total = out_ref
-    copies = []
-    for g in range(RADIX_A // 4):
-        part = pl.ds(4 * g, 4)
-        copies.append(pltpu.make_async_copy(w_hbm.at[part], w_ref.at[part], sems.at[g]))
-        copies[g].start()
-    waited = 0
-    beam_count = w_ref.shape[1]
+        out_hbm, total, far_ref, sems, out_sem = refs
+    size = far_ref.shape[0] // sems.shape[0]
+    parts = [pl.ds(i * size, size) for i in range(sems.shape[0])]
+    copies = fetch([(far_hbm.at[part], far_ref.at[part]) for part in parts], sems)
+    if last:
+        early_copy.start()
+    here = False
+    beam_count = near_ref.shape[1]
     spectra = total.shape[0] // (2 * RADIX_A)
-    if last:
-        early = early_ref.shape[0] // (2 * RADIX_A)
-        for t in range(early):
-            for row in range(0, 2 * RADIX_A, 8):
-                total[pl.ds((row + 1) * spectra - early + t, 8, stride=spectra), :] = early_ref[
-                    pl.ds(row * early + t, 8, stride=early), :
-                ]
     lane = lax.broadcasted_iota(jnp.int32, (1, 128), 1)
     even = (lax.broadcasted_iota(jnp.int32, (1, 8, 128), 1) & 1) == 0
     for group in range(quads):
@@ -435,10 +439,16 @@
         c1 = (base + lane) // (16 * quads) * 4 + lane % 8 // 2
         real = imag = None
         for g in range(low, high + 1):
-            while waited <= g:
-                copies[waited].wait()
-                waited += 1
-            weights = w_ref[4 * g : 4 * g + 4].reshape(4 * beam_count, 1024)
+            first = 4 * g
+            if first < KEPT:
+                weights = near_ref[first : first + 4]
+            else:
+                if not here:
+                    for copy in copies:
+                        copy.wait()
+                    here = True
+                weights = far_ref[first - KEPT : first - KEPT + 4]
+            weights = weights.reshape(4 * beam_count, 1024)
             got = jnp.dot(weights, data, preferred_element_type=F32)
             for c in range(4):
                 piece = got[beam_count * c : beam_count * (c + 1)]
@@ -455,29 +465,39 @@
             t = at % (16 * quads) // 16 * PAIR + at % 16 // 8
             total[pl.ds(block * 8 * spectra + t, 8, stride=spectra), :] = turned[m : m + 8]
     if last:
+        early_copy.wait()
+        early = early_ref.shape[0] // (2 * RADIX_A)
+        for t in range(early):
+            for row in range(0, 2 * RADIX_A, 8):
+                total[pl.ds((row + 1) * spectra - early + t, 8, stride=spectra), :] = early_ref[
+                    pl.ds(row * early + t, 8, stride=early), :
+                ]
         out_ref[...] = total[...].astype(BF16)
+    else:
+        out_copy = pltpu.make_async_copy(total, out_hbm, out_sem)
+        out_copy.start()
+        out_copy.wait()
 
 
 def beams(received, weights, quads, early):
     count = quads * QUAD // 2
     received = received.reshape(RADIX_B, quads, 8, 128)
-    operands = [received, in_hbm(weights)]
-    in_specs = [IN_VMEM, IN_HBM]
-    scratch = [pltpu.VMEM(weights.shape, BF16), pltpu.SemaphoreType.DMA((RADIX_A // 4,))]
+    kept, others = weights
+    operands = [received, pltpu.with_memory_space_constraint(kept, pltpu.VMEM), in_hbm(others)]
+    in_specs = [IN_VMEM, IN_VMEM, IN_HBM]
     last = early is not None
-    if last:
-        operands.append(early)
-        in_specs.append(IN_VMEM)
-        shape = (2 * RADIX_A * count + early.shape[0], 128)
-        out_shape = jax.ShapeDtypeStruct(shape, BF16)
-        scratch = [pltpu.VMEM(shape, F32)] + scratch
-    else:
-        out_shape = jax.ShapeDtypeStruct((2 * RADIX_A * count, 128), F32)
+    shape = (2 * RADIX_A * count + (early.shape[0] if last else 0), 128)
+    scratch = [pltpu.VMEM(shape, F32), pltpu.VMEM(others.shape, BF16), pltpu.SemaphoreType.DMA((8,))]
+    if last:
+        operands.append(in_hbm(early))
+        in_specs.append(IN_HBM)
+        scratch += [pltpu.VMEM(early.shape, F32)]
+    scratch += [pltpu.SemaphoreType.DMA]
     return pl.pallas_call(
         functools.partial(beams_body, quads, last),
-        out_shape=out_shape,
+        out_shape=jax.ShapeDtypeStruct(shape, BF16) if last else pltpu.HBM(shape, F32),
         in_specs=in_specs,
-        out_specs=IN_VMEM,
+        out_specs=IN_VMEM if last else IN_HBM,
         scratch_shapes=scratch,
         compiler_params=params(),
         cost_estimate=LIGHT,
@@ -497,23 +517,23 @@
     x = x.transpose(0, 1, 3, 2, 4).reshape(stations, 2, frames * ROWS, RADIX_B)
     pairs = [(i, i + 1) for i in range(size - 1)]
     lead = stations - 1
-    rest = frames - TAPS + 1, TAPS - 2
-    parts = [(0, stations, frames - 1, 1), (0, lead, *rest), (lead, 1, *rest)]
+    rest = frames - TAPS + 1, TAPS - 1 - NEAR
+    parts = [(0, stations, frames - NEAR, NEAR), (0, lead, *rest), (lead, 1, *rest)]
     near, far, far_last, taps2 = history(x, parts, taps)
     near = lax.ppermute(near, "tm", pairs)
     far = lax.ppermute(far, "tm", pairs)
 
     tables = (jnp.asarray(outer_table()), jnp.asarray(twiddles()), jnp.asarray(inner_table()))
     late = frames - EARLY
-    filtered = filter_first(x, taps2, late + 1, EARLY - 1)
+    filtered = filter_first(x, taps2, late + NEAR, EARLY - NEAR)
+    filtered, far_last = lax.optimization_barrier((filtered, far_last))
     early_sent = channelise_early(x, near, taps2, filtered, tables, late, EARLY)
-    early_sent, far_last = lax.optimization_barrier((early_sent, far_last))
     early_got = turn(early_sent)
     far_last = lax.ppermute(far_last, "tm", pairs)
     upper = lax.axis_index("stn").astype(jnp.int32).reshape(1)
     weights = beam_weights(upper, codes, flags)
     ahead = channelise_late(x, near, far, taps2, tables, 0, late)
-    main_sent = channelise_late(x, near, far_last, taps2, tables, lead, late, ahead)
+    main_sent = channelise_late(x[lead:, :, : late * ROWS], near, far_last, taps2, tables, lead, late, ahead)
     main_got = turn(main_sent)
     early = beams(early_got, weights, EARLY // PAIR, None)
     result = beams(main_got, weights, late // PAIR, early)

time: 107 us -> 105 us (0.981)
  local copies, waits for them, and re-layouts: 1.71 us -> 3.62 us
  Pallas kernels: 33.5 us -> 31.9 us
  waiting for transfers between devices: 39.7 us -> 38.3 us
    ppermute x1, waiting for transfers between devices: 12 us -> 4.28 us  [shards(): far_last = lax.ppermute(far_last, 'tm', pairs)]
    all_to_all x2, waiting for transfers between devices: 24.5 us -> 30.5 us  [turn(): lax.all_to_all(spectra, 'stn', split_axis=0, concat_axis=0, tiled=True)]
    pallas_call x3, Pallas kernels: 18.8 us -> 15.1 us  [the longest x2 8.5 us: beams(): pl.pallas_call(functools.partial(beams_body, quads, last), out_shape=jax....]
    pallas_call x2, Pallas kernels: 6.79 us -> 8.95 us  [channelise_late(): pl.pallas_call(functools.partial(late_body, last, count, quads, base, sta...]
    ppermute x1, waiting for transfers between devices: 0.13 us -> 1.78 us  [shards(): far = lax.ppermute(far, 'tm', pairs)]
    ppermute x1, waiting for transfers between devices: 3.08 us -> 1.73 us  [shards(): near = lax.ppermute(near, 'tm', pairs)]
    unnamed x11 -> x15, local copies, waits for them, and re-layouts: 1.05 us -> 2.22 us
where the time goes in v4:
time: 105 us
  waiting for transfers between devices  38.3 us (36%)
  Pallas kernels  31.9 us (30%)
  starting transfers between devices  30.6 us (29%)
  local copies, waits for them, and re-layouts  3.62 us (3%)
    all_to_all x2, waiting for transfers between devices, turn(): lax.all_to_all(spectra, 'stn', split_axis=0, concat_axis=0, tiled=True)  30.5 us
    all_to_all x2, starting transfers between devices, turn(): lax.all_to_all(spectra, 'stn', split_axis=0, concat_axis=0, tiled=True)  26.7 us
    pallas_call x2, Pallas kernels, channelise_late(): pl.pallas_call(functools.partial(late_body, last, count, quads, base, sta...  8.95 us
    pallas_call x2, Pallas kernels, beams(): pl.pallas_call(functools.partial(beams_body, quads, last), out_shape=jax....  8.5 us
    pallas_call x1, Pallas kernels, beam_weights(): pl.pallas_call(weights_body, out_shape=[pltpu.VMEM((KEPT,) + shape[1:], B...  6.59 us
    ppermute x1, waiting for transfers between devices, shards(): far_last = lax.ppermute(far_last, 'tm', pairs)  4.28 us
    pallas_call x1, Pallas kernels, channelise_early(): pl.pallas_call(functools.partial(early_body, first, count, quads, station...  3.13 us
    pallas_call x1, Pallas kernels, history(): pl.pallas_call(functools.partial(history_body, starts), out_shape=out_sha...  2.42 us
  transfers between devices with their start and end apart: 5, of which 5 were waited for; matrix products, arithmetic and copies ran while one was open for 1% of the time, Pallas kernels for 24%

profile of v4, /device:TPU:7, one launch (start us, length us, event | category | flops | bytes accessed | tf_op | source)
XLA Modules:
  0.0 104.6 jit_solution(5927310839879503006)
XLA Ops:
  0.0 2.4 %shard_map.73 = (bf16[4,2,64,128]{3,2,1,0:T(8,128)(2,1)}, bf16[3,2,640,128]{3,2,1,0:T(8,128)(2,1)}, bf16[1,2,640,128]{3,2,1,0:T(8,128)(2,1)}, f32[12,64,128]{2,1,0:T(8,128)S(1)}) custom-call(bf16[4,2,1024,128]{3,2,1,0:T(8,128)(2,1)} %bitcast.12, f32[12,4096]{1,0:T(8,128)} %refs_0_.1), custom_call_target="tpu_custom_call" | custom-call | flops 1024 | bytes 1024 | tf_op jit(solution)/shard_map/pallas_call | solution.py:354
  2.4 1.3 %collective-permute-start = (bf16[4,2,64,128]{3,2,1,0:T(8,128)(2,1)}, bf16[4,2,64,128]{3,2,1,0:T(8,128)(2,1)S(1)}, u32[]{:S(2)}, u32[]{:S(2)}) collective-permute-start(bf16[4,2,64,128]{3,2,1,0:T(8,128)(2,1)} %get-tuple-element.13), channel_id=1, source_target_pairs={{0,1},{2,3},{4,5},{6,7},{8,9},{10,11},{12,13},{14,15},{16,17},{18,... | collective-permute-start | bytes 393224 | tf_op jit(solution)/shard_map/ppermute | solution.py:523
  3.7 1.3 %collective-permute-start.2 = (bf16[3,2,640,128]{3,2,1,0:T(8,128)(2,1)}, bf16[3,2,640,128]{3,2,1,0:T(8,128)(2,1)}, u32[]{:S(2)}, u32[]{:S(2)}) collective-permute-start(bf16[3,2,640,128]{3,2,1,0:T(8,128)(2,1)} %get-tuple-element.17), channel_id=1, source_target_pairs={{0,1},{2,3},{4,5},{6,7},{8,9},{10,11},{12,13},{14,15},{16,17},{18,... | collective-permute-start | bytes 2949128 | tf_op jit(solution)/shard_map/ppermute | solution.py:524
  5.0 0.0 copy-done
  5.0 0.0 copy-start.6
  5.1 2.3 %shard_map.74.before = bf16[2560,128]{1,0:T(8,128)(2,1)S(1)} custom-call(bf16[4,2,1024,128]{3,2,1,0:T(8,128)(2,1)S(1)} %bitcast.14, f32[12,64,128]{2,1,0:T(8,128)S(1)} %get-tuple-element.14.taps2), custom_call_target="tpu_custom_call" | custom-call | flops 137438953472 | bytes 1024 | tf_op jit(solution)/shard_map/pallas_call | solution.py:249
  7.3 0.0 copy-done.6
  7.3 1.3 %collective-permute-start.1 = (bf16[1,2,640,128]{3,2,1,0:T(8,128)(2,1)S(1)}, bf16[1,2,640,128]{3,2,1,0:T(8,128)(2,1)S(1)}, u32[]{:S(2)}, u32[]{:S(2)}) collective-permute-start(bf16[1,2,640,128]{3,2,1,0:T(8,128)(2,1)S(1)} %copy-done.6), channel_id=1, source_target_pairs={{0,1},{2,3},{4,5},{6,7},{8,9},{10,11},{12,13},{14,15},{16,17},{18,... | collective-permute-start | bytes 983048 | tf_op jit(solution)/shard_map/ppermute | solution.py:532
  8.7 1.7 %collective-permute-done.near_ref = bf16[4,2,64,128]{3,2,1,0:T(8,128)(2,1)S(1)} collective-permute-done((bf16[4,2,64,128]{3,2,1,0:T(8,128)(2,1)}, bf16[4,2,64,128]{3,2,1,0:T(8,128)(2,1)S(1)}, u32[]{:S(2)}, u32[]{:S(2)}) %collective-permute-start) | collective-permute-done | bytes 131104 | tf_op jit(solution)/shard_map/ppermute | solution.py:523
  10.4 3.1 %shard_map.78 = bf16[3072,128]{1,0:T(8,128)(2,1)} custom-call(bf16[4,2,1024,128]{3,2,1,0:T(8,128)(2,1)S(1)} %bitcast.16, bf16[4,2,64,128]{3,2,1,0:T(8,128)(2,1)S(1)} %collective-permute-done.near_ref, f32[12,64,128]{2,1,0:T(8,128)S(1)} %get-tuple-element.14.taps2, bf16[2560,128]{1,0:T(8,128)(2,1)S(1)} %shard_map.74.before, ...), custom_call_target="tpu_custom_call" | custom-call | flops 7516192768 | bytes 1024 | tf_op jit(solution)/shard_map/pallas_call | solution.py:263
  13.5 16.2 %all-to-all-start.1 = ((bf16[128,24,128]{2,1,0:T(8,128)(2,1)}), bf16[128,24,128]{2,1,0:T(8,128)(2,1)S(1)}, u32[]{:S(2)}, u32[]{:S(2)}) async-start(bf16[128,24,128]{2,1,0:T(8,128)(2,1)} %bitcast.21), calls=%async_computation.1 | async-start | bytes 1572864 | tf_op jit(solution)/shard_map/all_to_all | solution.py:509
  29.8 1.8 %collective-permute-done.2.far_ref = bf16[3,2,640,128]{3,2,1,0:T(8,128)(2,1)} collective-permute-done((bf16[3,2,640,128]{3,2,1,0:T(8,128)(2,1)}, bf16[3,2,640,128]{3,2,1,0:T(8,128)(2,1)}, u32[]{:S(2)}, u32[]{:S(2)}) %collective-permute-start.2) | collective-permute-done | bytes 983072 | tf_op jit(solution)/shard_map/ppermute | solution.py:524
  31.6 5.9 %shard_map.75.refs_0_ = f32[5120,128]{1,0:T(8,128)S(1)} custom-call(bf16[4,2,1024,128]{3,2,1,0:T(8,128)(2,1)} %bitcast.13, bf16[4,2,64,128]{3,2,1,0:T(8,128)(2,1)S(1)} %collective-permute-done.near_ref, bf16[3,2,640,128]{3,2,1,0:T(8,128)(2,1)} %collective-permute-done.2.far_ref, f32[12,64,128]{2,1,0:T(8,128)S(1)} %get-tuple-element.14.taps2, ...), custom_call_target="tpu_custom_call" | custom-call | flops 1024 | bytes 1024 | tf_op jit(solution)/shard_map/pallas_call | solution.py:300
  37.5 4.3 %collective-permute-done.1.far_ref = bf16[1,2,640,128]{3,2,1,0:T(8,128)(2,1)S(1)} collective-permute-done((bf16[1,2,640,128]{3,2,1,0:T(8,128)(2,1)S(1)}, bf16[1,2,640,128]{3,2,1,0:T(8,128)(2,1)S(1)}, u32[]{:S(2)}, u32[]{:S(2)}) %collective-permute-start.1) | collective-permute-done | bytes 327712 | tf_op jit(solution)/shard_map/ppermute | solution.py:532
  41.8 3.0 %shard_map.76 = bf16[5120,128]{1,0:T(8,128)(2,1)} custom-call(bf16[1,2,640,128]{3,2,1,0:T(8,128)(2,1)S(1)} %slice.4.x_ref, bf16[4,2,64,128]{3,2,1,0:T(8,128)(2,1)S(1)} %collective-permute-done.near_ref, bf16[1,2,640,128]{3,2,1,0:T(8,128)(2,1)S(1)} %collective-permute-done.1.far_ref, f32[12,64,128]{2,1,0:T(8,128)S(1)} %get-tuple-element.14.taps2, ...), custom_call_target="tpu_custom_call" | custom-call | flops 137438953472 | bytes 1024 | tf_op jit(solution)/shard_map/pallas_call | solution.py:300
  44.8 0.0 copy-start.5
  44.8 0.0 copy-start.4
  44.8 9.4 %all-to-all-done.1 = bf16[128,24,128]{2,1,0:T(8,128)(2,1)S(1)} async-done(((bf16[128,24,128]{2,1,0:T(8,128)(2,1)}), bf16[128,24,128]{2,1,0:T(8,128)(2,1)S(1)}, u32[]{:S(2)}, u32[]{:S(2)}) %all-to-all-start.1) | async-done | bytes 786464 | tf_op jit(solution)/shard_map/all_to_all | solution.py:509
  54.2 10.5 %all-to-all-start = ((bf16[128,40,128]{2,1,0:T(8,128)(2,1)}), bf16[128,40,128]{2,1,0:T(8,128)(2,1)S(1)}, u32[]{:S(2)}, u32[]{:S(2)}) async-start(bf16[128,40,128]{2,1,0:T(8,128)(2,1)} %bitcast.20), calls=%async_computation | async-start | bytes 2621440 | tf_op jit(solution)/shard_map/all_to_all | solution.py:509
  64.7 0.0 copy-done.5
  64.7 0.1 broadcast_in_dim.7
  64.9 0.2 broadcast_in_dim_reshape.3.scale_ref
  65.1 0.1 copy.10
  65.2 0.2 broadcast_in_dim.6
  65.4 0.9 copy.11.codes_ref
  66.3 0.9 copy-done.3
  67.2 6.6 %shard_map.77 = (bf16[16,64,1024]{2,1,0:T(8,128)(2,1)S(1)}, bf16[16,64,1024]{2,1,0:T(8,128)(2,1)}) custom-call(s32[1]{0:T(128)} %bitcast.7.upper_ref, s32[64,1024]{1,0:T(8,128)S(1)} %copy-done.3, f32[1,1024]{1,0:T(1,128)S(1)} %broadcast_in_dim_reshape.3.scale_ref), custom_call_target="tpu_custom_call" | custom-call | flops 1024 | bytes 1024 | tf_op jit(solution)/shard_map/pallas_call | solution.py:404
  73.8 0.0 copy-start.2
  73.8 1.1 %copy-done.2 = bf16[128,24,128]{2,1,0:T(8,128)(2,1)S(1)} copy-done((bf16[128,24,128]{2,1,0:T(8,128)(2,1)S(1)}, bf16[128,24,128]{2,1,0:T(8,128)(2,1)}, u32[]{:S(2)}) %copy-start.2) | copy-done | bytes 786456
  75.0 4.2 %shard_map.79.refs_0_ = f32[384,128]{1,0:T(8,128)} custom-call(bf16[128,3,8,128]{3,2,1,0:T(8,128)(2,1)S(1)} %bitcast.18, bf16[16,64,1024]{2,1,0:T(8,128)(2,1)S(1)} %get-tuple-element.18.near_ref, bf16[16,64,1024]{2,1,0:T(8,128)(2,1)} %get-tuple-element.19.far_hbm), custom_call_target="tpu_custom_call" | custom-call | flops 1024 | bytes 1024 | tf_op jit(solution)/shard_map/pallas_call | solution.py:496
  79.2 21.1 %all-to-all-done = bf16[128,40,128]{2,1,0:T(8,128)(2,1)S(1)} async-done(((bf16[128,40,128]{2,1,0:T(8,128)(2,1)}), bf16[128,40,128]{2,1,0:T(8,128)(2,1)S(1)}, u32[]{:S(2)}, u32[]{:S(2)}) %all-to-all-start) | async-done | bytes 1310752 | tf_op jit(solution)/shard_map/all_to_all | solution.py:509
  100.3 4.3 %shard_map.80 = bf16[1024,128]{1,0:T(8,128)(2,1)} custom-call(bf16[128,5,8,128]{3,2,1,0:T(8,128)(2,1)S(1)} %bitcast.17, bf16[16,64,1024]{2,1,0:T(8,128)(2,1)S(1)} %get-tuple-element.18.near_ref, bf16[16,64,1024]{2,1,0:T(8,128)(2,1)} %get-tuple-element.19.far_hbm, f32[384,128]{1,0:T(8,128)} %shard_map.79.refs_0_), custom_call_target="tpu_custom_call" | custom-call | flops 1024 | bytes 1024 | tf_op jit(solution)/shard_map/pallas_call | solution.py:496
  (7 shorter events, 0.0 us)
Async XLA Ops:
  0.0 5.0 %copy-start = (bf16[4,2,2,65536]{3,2,1,0:T(2,128)(2,1)S(1)}, bf16[4,2,2,65536]{3,2,1,0:T(2,128)(2,1)}, u32[]{:S(2)}) copy-start(bf16[4,2,2,65536]{3,2,1,0:T(2,128)(2,1)} %param.7) | copy-start | bytes 6291460
  2.4 8.0 %collective-permute-start = (bf16[4,2,64,128]{3,2,1,0:T(8,128)(2,1)}, bf16[4,2,64,128]{3,2,1,0:T(8,128)(2,1)S(1)}, u32[]{:S(2)}, u32[]{:S(2)}) collective-permute-start(bf16[4,2,64,128]{3,2,1,0:T(8,128)(2,1)} %get-tuple-element.13), channel_id=1, source_target_pairs={{0,1},{2,3},{4,5},{6,7},{8,9},{10,11},{12,13},{14,15},{16,17},{18,... | collective-permute-start | bytes 393224 | tf_op jit(solution)/shard_map/ppermute | solution.py:523
  3.7 27.8 %collective-permute-start.2 = (bf16[3,2,640,128]{3,2,1,0:T(8,128)(2,1)}, bf16[3,2,640,128]{3,2,1,0:T(8,128)(2,1)}, u32[]{:S(2)}, u32[]{:S(2)}) collective-permute-start(bf16[3,2,640,128]{3,2,1,0:T(8,128)(2,1)} %get-tuple-element.17), channel_id=1, source_target_pairs={{0,1},{2,3},{4,5},{6,7},{8,9},{10,11},{12,13},{14,15},{16,17},{18,... | collective-permute-start | bytes 2949128 | tf_op jit(solution)/shard_map/ppermute | solution.py:524
  5.0 2.3 %copy-start.6 = (bf16[1,2,640,128]{3,2,1,0:T(8,128)(2,1)S(1)}, bf16[1,2,640,128]{3,2,1,0:T(8,128)(2,1)}, u32[]{:S(2)}) copy-start(bf16[1,2,640,128]{3,2,1,0:T(8,128)(2,1)} %get-tuple-element.16) | copy-start | bytes 983044
  7.3 34.4 %collective-permute-start.1 = (bf16[1,2,640,128]{3,2,1,0:T(8,128)(2,1)S(1)}, bf16[1,2,640,128]{3,2,1,0:T(8,128)(2,1)S(1)}, u32[]{:S(2)}, u32[]{:S(2)}) collective-permute-start(bf16[1,2,640,128]{3,2,1,0:T(8,128)(2,1)S(1)} %copy-done.6), channel_id=1, source_target_pairs={{0,1},{2,3},{4,5},{6,7},{8,9},{10,11},{12,13},{14,15},{16,17},{18,... | collective-permute-start | bytes 983048 | tf_op jit(solution)/shard_map/ppermute | solution.py:532
  13.5 40.7 %all-to-all-start.1 = ((bf16[128,24,128]{2,1,0:T(8,128)(2,1)}), bf16[128,24,128]{2,1,0:T(8,128)(2,1)S(1)}, u32[]{:S(2)}, u32[]{:S(2)}) async-start(bf16[128,24,128]{2,1,0:T(8,128)(2,1)} %bitcast.21), calls=%async_computation.1 | async-start | bytes 1572864 | tf_op jit(solution)/shard_map/all_to_all | solution.py:509
  44.8 19.9 %copy-start.5 = (s32[512]{0:T(512)S(1)}, s32[512]{0:T(512)}, u32[]{:S(2)}) copy-start(s32[512]{0:T(512)} %param.10) | copy-start | bytes 6148
  44.8 20.2 %copy-start.4 = (s32[64,512]{1,0:T(8,128)S(1)}, s32[64,512]{1,0:T(8,128)}, u32[]{:S(2)}) copy-start(s32[64,512]{1,0:T(8,128)} %param.9) | copy-start | bytes 393220
  54.2 11.1 %copy-start.1 = (bf16[128,24,128]{2,1,0:T(8,128)(2,1)}, bf16[128,24,128]{2,1,0:T(8,128)(2,1)S(1)}, u32[]{:S(2)}) copy-start(bf16[128,24,128]{2,1,0:T(8,128)(2,1)S(1)} %all-to-all-done.1) | copy-start | bytes 2359300
  54.2 46.1 %all-to-all-start = ((bf16[128,40,128]{2,1,0:T(8,128)(2,1)}), bf16[128,40,128]{2,1,0:T(8,128)(2,1)S(1)}, u32[]{:S(2)}, u32[]{:S(2)}) async-start(bf16[128,40,128]{2,1,0:T(8,128)(2,1)} %bitcast.20), calls=%async_computation | async-start | bytes 2621440 | tf_op jit(solution)/shard_map/all_to_all | solution.py:509
  66.3 0.9 copy-start.3
  73.8 1.1 %copy-start.2 = (bf16[128,24,128]{2,1,0:T(8,128)(2,1)S(1)}, bf16[128,24,128]{2,1,0:T(8,128)(2,1)}, u32[]{:S(2)}) copy-start(bf16[128,24,128]{2,1,0:T(8,128)(2,1)} %copy-done.1) | copy-start | bytes 2359300

commit v5 on v4

--- a/solution.py
+++ b/solution.py
@@ -204,8 +204,8 @@
 ):
     copies = fetch([(outer_hbm, outer_ref), (tw_hbm, tw_ref), (inner_hbm, inner_ref)], in_sems)
     fir(first, NEAR, 0, stations, x_ref, near_ref, None, taps2, filt, lambda s, pol, t: (s * 2 + pol) * NEAR + t)
-    for copy in copies:
-        copy.wait()
+    copies[0].wait()
+    copies[1].wait()
 
     def frame(s, pol, t):
         if t < NEAR:
@@ -213,18 +213,22 @@
         return rows_of(before, (s * 2 + pol) * (count - NEAR) + t - NEAR)
 
     outer_stage(quads, stations, frame, outer_ref, tw_ref, mid)
+    copies[2].wait()
     for s in range(stations):
         inner_stage(quads, s, mid, s * 128 * quads, inner_ref, turn)
     send_out(turn, packed, out_ref, sems)
 
 
 def late_body(
-    last, count, quads, base, stations, x_ref, near_ref, far_ref, taps2, outer_hbm, tw_hbm, inner_hbm, *refs
+    last, count, quads, base, stations, x_ref, near_ref, far_ref, taps2, outer, tw, inner, *refs
 ):
     if last:
-        before, out_ref, outer_ref, tw_ref, inner_ref, filt, mid, in_sems, turn, packed, sems = refs
+        before, out_ref, filt, mid, turn, packed, sems = refs
+        copies = []
     else:
-        turn, outer_ref, tw_ref, inner_ref, filt, mid, in_sems, held, held_sem = refs
+        turn, *tables, filt, mid, in_sems, held, held_sem = refs
+        copies = fetch(list(zip((outer, tw, inner), tables)), in_sems)
+        outer, tw, inner = tables
         copy = pltpu.make_async_copy(x_ref.at[pl.ds(base, stations), :, pl.ds(0, held.shape[2])], held, held_sem)
         copy.start()
         copy.wait()
@@ -233,13 +237,12 @@
     def place(s, pol, t):
         return (s * 2 + pol) * count + t
 
-    copies = fetch([(outer_hbm, outer_ref), (tw_hbm, tw_ref), (inner_hbm, inner_ref)], in_sems)
     fir(0, count, base, stations, x_ref, near_ref, far_ref, taps2, filt, place)
     for copy in copies:
         copy.wait()
-    outer_stage(quads, stations, lambda *at: rows_of(filt, place(*at)), outer_ref, tw_ref, mid)
+    outer_stage(quads, stations, lambda *at: rows_of(filt, place(*at)), outer, tw, mid)
     for s in range(stations):
-        inner_stage(quads, base + s, mid, s * 128 * quads, inner_ref, turn)
+        inner_stage(quads, base + s, mid, s * 128 * quads, inner, turn)
     if last:
         send_out(turn, packed, out_ref, sems, before, base)
 
@@ -284,10 +287,9 @@
     quads = 2 * count // QUAD
     rows = RADIX_B * 8 * quads
     last = before is not None
-    scratch = [pltpu.VMEM(table.shape, table.dtype) for table in tables] + [
+    scratch = [
         pltpu.VMEM((stations * 2 * count * ROWS, RADIX_B), BF16),
         pltpu.VMEM((stations * 128 * quads, 2 * RADIX_B), BF16),
-        pltpu.SemaphoreType.DMA((3,)),
     ]
     if last:
         scratch += [
@@ -295,17 +297,26 @@
             pltpu.VMEM((rows, 128), BF16),
             pltpu.SemaphoreType.DMA((8,)),
         ]
+        out_shape = pltpu.HBM((rows, 128), BF16)
     else:
-        scratch += [pltpu.VMEM((stations, 2, count * ROWS, RADIX_B), BF16), pltpu.SemaphoreType.DMA]
+        scratch += [
+            pltpu.SemaphoreType.DMA((3,)),
+            pltpu.VMEM((stations, 2, count * ROWS, RADIX_B), BF16),
+            pltpu.SemaphoreType.DMA,
+        ]
+        out_shape = [jax.ShapeDtypeStruct((rows, 128), F32)]
+        out_shape += [jax.ShapeDtypeStruct(table.shape, table.dtype) for table in tables]
+        x, tables = in_hbm(x), tuple(map(in_hbm, tables))
+    home = IN_VMEM if last else IN_HBM
     return pl.pallas_call(
         functools.partial(late_body, last, count, quads, base, stations),
-        out_shape=pltpu.HBM((rows, 128), BF16) if last else jax.ShapeDtypeStruct((rows, 128), F32),
-        in_specs=[IN_VMEM if last else IN_HBM] + [IN_VMEM] * 3 + [IN_HBM] * 3 + [IN_VMEM] * last,
-        out_specs=IN_HBM if last else IN_VMEM,
+        out_shape=out_shape,
+        in_specs=[home] + [IN_VMEM] * 3 + [home] * 3 + [IN_VMEM] * last,
+        out_specs=IN_HBM if last else [IN_VMEM] * 4,
         scratch_shapes=scratch,
         compiler_params=params(),
         cost_estimate=HEAVY if last else LIGHT,
-    )(x if last else in_hbm(x), near, far, taps2, *map(in_hbm, tables), *([before] if last else []))
+    )(x, near, far, taps2, *tables, *([before] if last else []))
 
 
 def history_body(starts, x_ref, *refs):
@@ -532,7 +543,7 @@
     far_last = lax.ppermute(far_last, "tm", pairs)
     upper = lax.axis_index("stn").astype(jnp.int32).reshape(1)
     weights = beam_weights(upper, codes, flags)
-    ahead = channelise_late(x, near, far, taps2, tables, 0, late)
+    ahead, *tables = channelise_late(x, near, far, taps2, tables, 0, late)
     main_sent = channelise_late(x[lead:, :, : late * ROWS], near, far_last, taps2, tables, lead, late, ahead)
     main_got = turn(main_sent)
     early = beams(early_got, weights, EARLY // PAIR, None)

time: 105 us -> 105 us (level)
    unnamed x15 -> x13, local copies, waits for them, and re-layouts: 2.22 us -> 2.22 us
where the time goes in v5:
time: 105 us; the launch traced here: 104 us
  waiting for transfers between devices  38.3 us (36%)
  Pallas kernels  31.9 us (30%)
  starting transfers between devices  30.3 us (29%)
  local copies, waits for them, and re-layouts  3.62 us (3%)
    all_to_all x2, waiting for transfers between devices, turn(): lax.all_to_all(spectra, 'stn', split_axis=0, concat_axis=0, tiled=True)  30.8 us
    all_to_all x2, starting transfers between devices, turn(): lax.all_to_all(spectra, 'stn', split_axis=0, concat_axis=0, tiled=True)  26.5 us
    pallas_call x2, Pallas kernels, channelise_late(): pl.pallas_call(functools.partial(late_body, last, count, quads, base, sta...  8.94 us
    pallas_call x2, Pallas kernels, beams(): pl.pallas_call(functools.partial(beams_body, quads, last), out_shape=jax....  8.49 us
    pallas_call x1, Pallas kernels, beam_weights(): pl.pallas_call(weights_body, out_shape=[pltpu.VMEM((KEPT,) + shape[1:], B...  6.59 us
    ppermute x1, waiting for transfers between devices, shards(): far_last = lax.ppermute(far_last, 'tm', pairs)  4.09 us
    pallas_call x1, Pallas kernels, channelise_early(): pl.pallas_call(functools.partial(early_body, first, count, quads, station...  3.19 us
    pallas_call x1, Pallas kernels, history(): pl.pallas_call(functools.partial(history_body, starts), out_shape=out_sha...  2.42 us
  transfers between devices with their start and end apart: 5, of which 5 were waited for; matrix products, arithmetic and copies ran while one was open for 1% of the time, Pallas kernels for 24%

profile of v5, /device:TPU:7, one launch (start us, length us, event | category | flops | bytes accessed | tf_op | source)
XLA Modules:
  0.0 104.4 jit_solution(12126536230536470893)
XLA Ops:
  0.0 2.4 %shard_map.73 = (bf16[4,2,64,128]{3,2,1,0:T(8,128)(2,1)}, bf16[3,2,640,128]{3,2,1,0:T(8,128)(2,1)}, bf16[1,2,640,128]{3,2,1,0:T(8,128)(2,1)}, f32[12,64,128]{2,1,0:T(8,128)S(1)}) custom-call(bf16[4,2,1024,128]{3,2,1,0:T(8,128)(2,1)} %bitcast.12, f32[12,4096]{1,0:T(8,128)} %refs_0_.1), custom_call_target="tpu_custom_call" | custom-call | flops 1024 | bytes 1024 | tf_op jit(solution)/shard_map/pallas_call | solution.py:365
  2.4 1.3 %collective-permute-start = (bf16[4,2,64,128]{3,2,1,0:T(8,128)(2,1)}, bf16[4,2,64,128]{3,2,1,0:T(8,128)(2,1)S(1)}, u32[]{:S(2)}, u32[]{:S(2)}) collective-permute-start(bf16[4,2,64,128]{3,2,1,0:T(8,128)(2,1)} %get-tuple-element.17), channel_id=1, source_target_pairs={{0,1},{2,3},{4,5},{6,7},{8,9},{10,11},{12,13},{14,15},{16,17},{18,... | collective-permute-start | bytes 393224 | tf_op jit(solution)/shard_map/ppermute | solution.py:534
  3.7 1.3 %collective-permute-start.2 = (bf16[3,2,640,128]{3,2,1,0:T(8,128)(2,1)}, bf16[3,2,640,128]{3,2,1,0:T(8,128)(2,1)}, u32[]{:S(2)}, u32[]{:S(2)}) collective-permute-start(bf16[3,2,640,128]{3,2,1,0:T(8,128)(2,1)} %get-tuple-element.21), channel_id=1, source_target_pairs={{0,1},{2,3},{4,5},{6,7},{8,9},{10,11},{12,13},{14,15},{16,17},{18,... | collective-permute-start | bytes 2949128 | tf_op jit(solution)/shard_map/ppermute | solution.py:535
  5.0 0.0 copy-done
  5.0 2.3 %shard_map.74.before = bf16[2560,128]{1,0:T(8,128)(2,1)S(1)} custom-call(bf16[4,2,1024,128]{3,2,1,0:T(8,128)(2,1)S(1)} %bitcast.14, f32[12,64,128]{2,1,0:T(8,128)S(1)} %get-tuple-element.18.taps2), custom_call_target="tpu_custom_call" | custom-call | flops 137438953472 | bytes 1024 | tf_op jit(solution)/shard_map/pallas_call | solution.py:252
  7.3 1.3 %collective-permute-start.1 = (bf16[1,2,640,128]{3,2,1,0:T(8,128)(2,1)}, bf16[1,2,640,128]{3,2,1,0:T(8,128)(2,1)S(1)}, u32[]{:S(2)}, u32[]{:S(2)}) collective-permute-start(bf16[1,2,640,128]{3,2,1,0:T(8,128)(2,1)} %get-tuple-element.20), channel_id=1, source_target_pairs={{0,1},{2,3},{4,5},{6,7},{8,9},{10,11},{12,13},{14,15},{16,17},{18,... | collective-permute-start | bytes 983048 | tf_op jit(solution)/shard_map/ppermute | solution.py:543
  8.7 1.7 %collective-permute-done.near_ref = bf16[4,2,64,128]{3,2,1,0:T(8,128)(2,1)S(1)} collective-permute-done((bf16[4,2,64,128]{3,2,1,0:T(8,128)(2,1)}, bf16[4,2,64,128]{3,2,1,0:T(8,128)(2,1)S(1)}, u32[]{:S(2)}, u32[]{:S(2)}) %collective-permute-start) | collective-permute-done | bytes 131104 | tf_op jit(solution)/shard_map/ppermute | solution.py:534
  10.4 3.2 %shard_map.78 = bf16[3072,128]{1,0:T(8,128)(2,1)} custom-call(bf16[4,2,1024,128]{3,2,1,0:T(8,128)(2,1)S(1)} %bitcast.16, bf16[4,2,64,128]{3,2,1,0:T(8,128)(2,1)S(1)} %collective-permute-done.near_ref, f32[12,64,128]{2,1,0:T(8,128)S(1)} %get-tuple-element.18.taps2, bf16[2560,128]{1,0:T(8,128)(2,1)S(1)} %shard_map.74.before, ...), custom_call_target="tpu_custom_call" | custom-call | flops 7516192768 | bytes 1024 | tf_op jit(solution)/shard_map/pallas_call | solution.py:266
  13.6 16.2 %all-to-all-start.1 = ((bf16[128,24,128]{2,1,0:T(8,128)(2,1)}), bf16[128,24,128]{2,1,0:T(8,128)(2,1)S(1)}, u32[]{:S(2)}, u32[]{:S(2)}) async-start(bf16[128,24,128]{2,1,0:T(8,128)(2,1)} %bitcast.21), calls=%async_computation.1 | async-start | bytes 1572864 | tf_op jit(solution)/shard_map/all_to_all | solution.py:520
  29.9 1.7 %collective-permute-done.2.far_ref = bf16[3,2,640,128]{3,2,1,0:T(8,128)(2,1)} collective-permute-done((bf16[3,2,640,128]{3,2,1,0:T(8,128)(2,1)}, bf16[3,2,640,128]{3,2,1,0:T(8,128)(2,1)}, u32[]{:S(2)}, u32[]{:S(2)}) %collective-permute-start.2) | collective-permute-done | bytes 983072 | tf_op jit(solution)/shard_map/ppermute | solution.py:535
  31.6 6.1 %shard_map.75 = (f32[5120,128]{1,0:T(8,128)S(1)}, bf16[256,256]{1,0:T(8,128)(2,1)S(1)}, f32[2,128,128]{2,1,0:T(8,128)S(1)}, bf16[256,256]{1,0:T(8,128)(2,1)S(1)}) custom-call(bf16[4,2,1024,128]{3,2,1,0:T(8,128)(2,1)} %bitcast.13, bf16[4,2,64,128]{3,2,1,0:T(8,128)(2,1)S(1)} %collective-permute-done.near_ref, ...), custom_call_target="tpu_custom_call" | custom-call | flops 1024 | bytes 1024 | tf_op jit(solution)/shard_map/pallas_call | solution.py:311
  37.7 4.1 %collective-permute-done.1.far_ref = bf16[1,2,640,128]{3,2,1,0:T(8,128)(2,1)S(1)} collective-permute-done((bf16[1,2,640,128]{3,2,1,0:T(8,128)(2,1)}, bf16[1,2,640,128]{3,2,1,0:T(8,128)(2,1)S(1)}, u32[]{:S(2)}, u32[]{:S(2)}) %collective-permute-start.1) | collective-permute-done | bytes 327712 | tf_op jit(solution)/shard_map/ppermute | solution.py:543
  41.8 2.8 %shard_map.76 = bf16[5120,128]{1,0:T(8,128)(2,1)} custom-call(bf16[1,2,640,128]{3,2,1,0:T(8,128)(2,1)S(1)} %slice.4.x_ref, bf16[4,2,64,128]{3,2,1,0:T(8,128)(2,1)S(1)} %collective-permute-done.near_ref, bf16[1,2,640,128]{3,2,1,0:T(8,128)(2,1)S(1)} %collective-permute-done.1.far_ref, f32[12,64,128]{2,1,0:T(8,128)S(1)} %get-tuple-element.18.taps2, ...), custom_call_target="tpu_custom_call" | custom-call | flops 137438953472 | bytes 1024 | tf_op jit(solution)/shard_map/pallas_call | solution.py:311
  44.6 0.0 copy-start.5
  44.6 0.0 copy-start.4
  44.6 9.6 %all-to-all-done.1 = bf16[128,24,128]{2,1,0:T(8,128)(2,1)S(1)} async-done(((bf16[128,24,128]{2,1,0:T(8,128)(2,1)}), bf16[128,24,128]{2,1,0:T(8,128)(2,1)S(1)}, u32[]{:S(2)}, u32[]{:S(2)}) %all-to-all-start.1) | async-done | bytes 786464 | tf_op jit(solution)/shard_map/all_to_all | solution.py:520
  54.3 10.2 %all-to-all-start = ((bf16[128,40,128]{2,1,0:T(8,128)(2,1)}), bf16[128,40,128]{2,1,0:T(8,128)(2,1)S(1)}, u32[]{:S(2)}, u32[]{:S(2)}) async-start(bf16[128,40,128]{2,1,0:T(8,128)(2,1)} %bitcast.20), calls=%async_computation | async-start | bytes 2621440 | tf_op jit(solution)/shard_map/all_to_all | solution.py:520
  64.5 0.0 copy-done.5
  64.5 0.1 broadcast_in_dim.7
  64.7 0.2 broadcast_in_dim_reshape.3.scale_ref
  64.8 0.0 copy-done.4
  64.9 0.1 copy.10
  65.0 0.2 broadcast_in_dim.6
  65.2 0.0 copy-done.1
  65.2 0.9 copy.11.codes_ref
  66.1 0.9 copy-done.3
  67.0 6.6 %shard_map.77 = (bf16[16,64,1024]{2,1,0:T(8,128)(2,1)S(1)}, bf16[16,64,1024]{2,1,0:T(8,128)(2,1)}) custom-call(s32[1]{0:T(128)} %bitcast.7.upper_ref, s32[64,1024]{1,0:T(8,128)S(1)} %copy-done.3, f32[1,1024]{1,0:T(1,128)S(1)} %broadcast_in_dim_reshape.3.scale_ref), custom_call_target="tpu_custom_call" | custom-call | flops 1024 | bytes 1024 | tf_op jit(solution)/shard_map/pallas_call | solution.py:415
  73.6 0.0 copy-start.2
  73.6 1.1 %copy-done.2 = bf16[128,24,128]{2,1,0:T(8,128)(2,1)S(1)} copy-done((bf16[128,24,128]{2,1,0:T(8,128)(2,1)S(1)}, bf16[128,24,128]{2,1,0:T(8,128)(2,1)}, u32[]{:S(2)}) %copy-start.2) | copy-done | bytes 786456
  74.8 4.2 %shard_map.79.refs_0_ = f32[384,128]{1,0:T(8,128)} custom-call(bf16[128,3,8,128]{3,2,1,0:T(8,128)(2,1)S(1)} %bitcast.18, bf16[16,64,1024]{2,1,0:T(8,128)(2,1)S(1)} %get-tuple-element.26.near_ref, bf16[16,64,1024]{2,1,0:T(8,128)(2,1)} %get-tuple-element.27.far_hbm), custom_call_target="tpu_custom_call" | custom-call | flops 1024 | bytes 1024 | tf_op jit(solution)/shard_map/pallas_call | solution.py:507
  79.0 21.1 %all-to-all-done = bf16[128,40,128]{2,1,0:T(8,128)(2,1)S(1)} async-done(((bf16[128,40,128]{2,1,0:T(8,128)(2,1)}), bf16[128,40,128]{2,1,0:T(8,128)(2,1)S(1)}, u32[]{:S(2)}, u32[]{:S(2)}) %all-to-all-start) | async-done | bytes 1310752 | tf_op jit(solution)/shard_map/all_to_all | solution.py:520
  100.1 4.3 %shard_map.80 = bf16[1024,128]{1,0:T(8,128)(2,1)} custom-call(bf16[128,5,8,128]{3,2,1,0:T(8,128)(2,1)S(1)} %bitcast.17, bf16[16,64,1024]{2,1,0:T(8,128)(2,1)S(1)} %get-tuple-element.26.near_ref, bf16[16,64,1024]{2,1,0:T(8,128)(2,1)} %get-tuple-element.27.far_hbm, f32[384,128]{1,0:T(8,128)} %shard_map.79.refs_0_), custom_call_target="tpu_custom_call" | custom-call | flops 1024 | bytes 1024 | tf_op jit(solution)/shard_map/pallas_call | solution.py:507
  (5 shorter events, 0.0 us)
Async XLA Ops:
  0.0 5.0 %copy-start = (bf16[4,2,2,65536]{3,2,1,0:T(2,128)(2,1)S(1)}, bf16[4,2,2,65536]{3,2,1,0:T(2,128)(2,1)}, u32[]{:S(2)}) copy-start(bf16[4,2,2,65536]{3,2,1,0:T(2,128)(2,1)} %param.7) | copy-start | bytes 6291460
  2.4 8.0 %collective-permute-start = (bf16[4,2,64,128]{3,2,1,0:T(8,128)(2,1)}, bf16[4,2,64,128]{3,2,1,0:T(8,128)(2,1)S(1)}, u32[]{:S(2)}, u32[]{:S(2)}) collective-permute-start(bf16[4,2,64,128]{3,2,1,0:T(8,128)(2,1)} %get-tuple-element.17), channel_id=1, source_target_pairs={{0,1},{2,3},{4,5},{6,7},{8,9},{10,11},{12,13},{14,15},{16,17},{18,... | collective-permute-start | bytes 393224 | tf_op jit(solution)/shard_map/ppermute | solution.py:534
  3.7 27.8 %collective-permute-start.2 = (bf16[3,2,640,128]{3,2,1,0:T(8,128)(2,1)}, bf16[3,2,640,128]{3,2,1,0:T(8,128)(2,1)}, u32[]{:S(2)}, u32[]{:S(2)}) collective-permute-start(bf16[3,2,640,128]{3,2,1,0:T(8,128)(2,1)} %get-tuple-element.21), channel_id=1, source_target_pairs={{0,1},{2,3},{4,5},{6,7},{8,9},{10,11},{12,13},{14,15},{16,17},{18,... | collective-permute-start | bytes 2949128 | tf_op jit(solution)/shard_map/ppermute | solution.py:535
  7.3 34.5 %collective-permute-start.1 = (bf16[1,2,640,128]{3,2,1,0:T(8,128)(2,1)}, bf16[1,2,640,128]{3,2,1,0:T(8,128)(2,1)S(1)}, u32[]{:S(2)}, u32[]{:S(2)}) collective-permute-start(bf16[1,2,640,128]{3,2,1,0:T(8,128)(2,1)} %get-tuple-element.20), channel_id=1, source_target_pairs={{0,1},{2,3},{4,5},{6,7},{8,9},{10,11},{12,13},{14,15},{16,17},{18,... | collective-permute-start | bytes 983048 | tf_op jit(solution)/shard_map/ppermute | solution.py:543
  13.6 40.7 %all-to-all-start.1 = ((bf16[128,24,128]{2,1,0:T(8,128)(2,1)}), bf16[128,24,128]{2,1,0:T(8,128)(2,1)S(1)}, u32[]{:S(2)}, u32[]{:S(2)}) async-start(bf16[128,24,128]{2,1,0:T(8,128)(2,1)} %bitcast.21), calls=%async_computation.1 | async-start | bytes 1572864 | tf_op jit(solution)/shard_map/all_to_all | solution.py:520
  44.6 19.9 %copy-start.5 = (s32[512]{0:T(512)S(1)}, s32[512]{0:T(512)}, u32[]{:S(2)}) copy-start(s32[512]{0:T(512)} %param.10) | copy-start | bytes 6148
  44.6 20.2 %copy-start.4 = (s32[64,512]{1,0:T(8,128)S(1)}, s32[64,512]{1,0:T(8,128)}, u32[]{:S(2)}) copy-start(s32[64,512]{1,0:T(8,128)} %param.9) | copy-start | bytes 393220
  54.3 10.9 %copy-start.1 = (bf16[128,24,128]{2,1,0:T(8,128)(2,1)}, bf16[128,24,128]{2,1,0:T(8,128)(2,1)S(1)}, u32[]{:S(2)}) copy-start(bf16[128,24,128]{2,1,0:T(8,128)(2,1)S(1)} %all-to-all-done.1) | copy-start | bytes 2359300
  54.3 45.8 %all-to-all-start = ((bf16[128,40,128]{2,1,0:T(8,128)(2,1)}), bf16[128,40,128]{2,1,0:T(8,128)(2,1)S(1)}, u32[]{:S(2)}, u32[]{:S(2)}) async-start(bf16[128,40,128]{2,1,0:T(8,128)(2,1)} %bitcast.20), calls=%async_computation | async-start | bytes 2621440 | tf_op jit(solution)/shard_map/all_to_all | solution.py:520
  66.1 0.9 copy-start.3
  73.6 1.1 %copy-start.2 = (bf16[128,24,128]{2,1,0:T(8,128)(2,1)S(1)}, bf16[128,24,128]{2,1,0:T(8,128)(2,1)}, u32[]{:S(2)}) copy-start(bf16[128,24,128]{2,1,0:T(8,128)(2,1)} %copy-done.1) | copy-start | bytes 2359300
